TPU v7x, 32 devices: a whole 2x2x4 slice. The times are simulated.
32 devices in a mesh: ew: 4 (over z), ns: 8 (over y, x, core).
Axes of the slice: x: 2, y: 2, z: 4, core: 2. Of those that a mesh axis runs over, the one named last changes fastest.
Arguments:
- tokens: bfloat16 [64, 128, 768], P('ns', 'ew'), may hold values from -16 to 16
- w_qkv: bfloat16 [768, 1152], replicated, may hold values from -0.21875 to 0.21875
- grad_out: bfloat16 [64, 128, 384], P('ns', 'ew'), may hold values from -6 to 6
Outputs:
- grad_tokens: bfloat16 [64, 128, 768], P('ns', 'ew')
- grad_w: bfloat16 [768, 1152], replicated
All inputs are finite; a program needn't handle non-finite values.
Results may differ from a plain program's by a relative error of at most 0.005.
The roundings to bfloat16 on the way count: a program that leaves them out, or rounds other values in their place, can miss the bound.
Values may be sent and summed in bfloat16 or wider, within the bound.
A program may use at most 64 MiB of HBM per device.

v0:
```python
import jax
import jax.numpy as jnp
from jax import lax
from jax.sharding import PartitionSpec as P

HEADS = 6
HDIM = 64
RADIUS = 6


def padded(value, sides, width):
    for axis, dim in sides:
        size, length = (lax.axis_size(axis), value.shape[dim])
        up = [(i, (i + 1) % size) for i in range(size - 1)]
        down = [(j, i) for i, j in up]
        last = lax.slice_in_dim(value, length - width, length, axis=dim)
        leading = lax.slice_in_dim(value, 0, width, axis=dim)
        before = lax.ppermute(last, axis, up)
        after = lax.ppermute(leading, axis, down)
        value = jnp.concatenate([before, value, after], axis=dim)
    return value


def build_mask(row_start, col_start, tile_rows, tile_cols, grid_rows, grid_cols):
    query_rows = jnp.arange(tile_rows, dtype=jnp.int32)
    key_rows = jnp.arange(tile_rows + 2 * RADIUS, dtype=jnp.int32)
    global_rows = row_start - RADIUS + key_rows
    row_ok = (
        (jnp.abs(query_rows[:, None] + RADIUS - key_rows[None, :]) <= RADIUS)
        & (global_rows >= 0)[None, :]
        & (global_rows < grid_rows)[None, :]
    )
    query_cols = jnp.arange(tile_cols, dtype=jnp.int32)
    key_cols = jnp.arange(tile_cols + 2 * RADIUS, dtype=jnp.int32)
    global_cols = col_start - RADIUS + key_cols
    col_ok = (
        (jnp.abs(query_cols[:, None] + RADIUS - key_cols[None, :]) <= RADIUS)
        & (global_cols >= 0)[None, :]
        & (global_cols < grid_cols)[None, :]
    )
    both = row_ok[:, None, :, None] & col_ok[None, :, None, :]
    return both.reshape(tile_rows * tile_cols, (tile_rows + 2 * RADIUS) * (tile_cols + 2 * RADIUS))


def local(tokens, w_qkv, grad_out):
    tile_rows, tile_cols, features = tokens.shape
    width = w_qkv.shape[1] // 3
    count = tile_rows * tile_cols
    flat_tokens = tokens.reshape(count, features)
    projected = jnp.dot(flat_tokens, w_qkv, preferred_element_type=jnp.float32).astype(jnp.bfloat16)
    queries = projected[:, :width]
    wide_kv = padded(
        projected[:, width:].reshape(tile_rows, tile_cols, 2 * width),
        (("ew", 1), ("ns", 0)),
        RADIUS,
    )
    ext_rows, ext_cols = (wide_kv.shape[0], wide_kv.shape[1])
    key_values = wide_kv.reshape(ext_rows * ext_cols, 2 * width)
    extent = ext_rows * ext_cols
    window = build_mask(
        lax.axis_index("ns") * tile_rows,
        lax.axis_index("ew") * tile_cols,
        tile_rows,
        tile_cols,
        lax.axis_size("ns") * tile_rows,
        lax.axis_size("ew") * tile_cols,
    )
    cotangent = grad_out.reshape(count, width)
    scaling = HDIM ** (-0.5)
    pair_width = 2 * HDIM
    query_parts, key_parts, value_parts = ([], [], [])
    for group in range(HEADS // 2):
        lower = group * pair_width
        query_pair = queries[:, lower : lower + pair_width].reshape(count, 2, HDIM)
        key_pair = key_values[:, lower : lower + pair_width].reshape(extent, 2, HDIM)
        value_pair = key_values[:, width + lower : width + lower + pair_width].reshape(
            extent, 2, HDIM
        )
        grad_pair = cotangent[:, lower : lower + pair_width].reshape(count, 2, HDIM)
        scores = (
            jnp.einsum("qhd,khd->hqk", query_pair, key_pair, preferred_element_type=jnp.float32)
            * scaling
        )
        scores = jnp.where(window[None], scores, -1e30)
        row_max = jnp.max(scores, axis=-1, keepdims=True)
        exp_scores = jnp.exp(scores - row_max)
        probs = exp_scores / jnp.sum(exp_scores, axis=-1, keepdims=True)
        probs_low = probs.astype(jnp.bfloat16)
        attended = jnp.einsum(
            "hqk,khd->qhd", probs_low, value_pair, preferred_element_type=jnp.float32
        )
        delta_row = jnp.transpose(jnp.sum(grad_pair.astype(jnp.float32) * attended, axis=-1))[
            :, :, None
        ]
        prob_grad = jnp.einsum(
            "qhd,khd->hqk", grad_pair, value_pair, preferred_element_type=jnp.float32
        )
        score_grad = (probs * (prob_grad - delta_row)).astype(jnp.bfloat16)
        query_parts.append(
            (
                jnp.einsum("hqk,khd->qhd", score_grad, key_pair, preferred_element_type=jnp.float32)
                * scaling
            ).reshape(count, pair_width)
        )
        key_parts.append(
            (
                jnp.einsum(
                    "hqk,qhd->khd", score_grad, query_pair, preferred_element_type=jnp.float32
                )
                * scaling
            ).reshape(extent, pair_width)
        )
        value_parts.append(
            jnp.einsum(
                "hqk,qhd->khd", probs_low, grad_pair, preferred_element_type=jnp.float32
            ).reshape(extent, pair_width)
        )
    query_grad = jnp.concatenate(query_parts, axis=1)
    ext_grads = jnp.concatenate(key_parts + value_parts, axis=1).reshape(
        ext_rows, ext_cols, 2 * width
    )
    side_strips = jnp.concatenate(
        [ext_grads[:, :RADIUS], ext_grads[:, tile_cols + RADIUS :]], axis=1
    )
    from_sides = padded(side_strips, (("ew", 1),), RADIUS)
    middle = ext_grads[:, RADIUS : tile_cols + RADIUS]
    middle = middle.at[:, :RADIUS].add(from_sides[:, :RADIUS])
    middle = middle.at[:, tile_cols - RADIUS :].add(from_sides[:, 3 * RADIUS :])
    edge_strips = jnp.concatenate([middle[:RADIUS], middle[tile_rows + RADIUS :]], axis=0)
    from_edges = padded(edge_strips, (("ns", 0),), RADIUS)
    owned = middle[RADIUS : tile_rows + RADIUS]
    owned = owned.at[:RADIUS].add(from_edges[:RADIUS])
    owned = owned.at[tile_rows - RADIUS :].add(from_edges[3 * RADIUS :])
    dqkv = jnp.concatenate([query_grad, owned.reshape(count, 2 * width)], axis=1).astype(
        jnp.bfloat16
    )
    grad_tokens = (
        jnp.dot(dqkv, w_qkv.T, preferred_element_type=jnp.float32)
        .astype(jnp.bfloat16)
        .reshape(tile_rows, tile_cols, features)
    )
    weight_part = lax.dot_general(
        flat_tokens, dqkv, (((0,), (0,)), ((), ())), preferred_element_type=jnp.float32
    )
    grad_w = lax.psum(weight_part, ("ew", "ns")).astype(jnp.bfloat16)
    return (grad_tokens, grad_w)


def solution(mesh):
    in_specs = (P("ns", "ew", None), P(), P("ns", "ew", None))
    out_specs = (P("ns", "ew", None), P())
    return jax.shard_map(local, mesh=mesh, in_specs=in_specs, out_specs=out_specs, check_vma=False)
```

profile of v0, /device:TPU:0, one launch (start us, length us, event | category | flops | bytes accessed | tf_op | source)
XLA Modules:
  0.0 227.7 jit_solution(4038875926624499870)
XLA Ops:
  0.6 1.5 copy-done
  2.1 1.7 convolution_convert_fusion
  3.9 4.9 %collective-permute-start = (bf16[8,6,768]{2,1,0:T(8,128)(2,1)S(1)}, bf16[8,6,768]{2,1,0:T(8,128)(2,1)S(1)}, u32[]{:S(2)}, u32[]{:S(2)}) collective-permute-start(bf16[8,6,768]{2,1,0:T(8,128)(2,1)S(1)} %get-tuple-element.69), channel_id=1, source_target_pairs={{0,8},{8,16},{16,24},{1,9},{9,17},{17,25},{2,10},{10,18},{18,26},{... | collective-permute-start | bytes 221192 | tf_op jit(solution)/shard_map/ppermute | solution.py:18
  8.9 1.3 collective-permute-start.1
  13.6 1.8 collective-permute-done.1
  16.4 2.0 collective-permute-start.2
  18.4 1.3 collective-permute-start.3
  23.2 1.5 pad_maximum_fusion
  24.7 1.4 reshape.354
  26.1 1.5 fusion.59
  30.7 2.9 %fusion.65 = (f32[2,256]{1,0:T(2,128)S(1)}, f32[2,256,880]{1,2,0:T(8,128)}) fusion(pred[256,880]{0,1:T(8,128)(4,1)} %copy.22, bf16[256,2,64]{0,2,1:T(8,128)(2,1)} %bitcast.145, bf16[880,2,64]{0,2,1:T(8,128)(2,1)S(1)} %bitcast.122), kind=kOutput, calls=%fused_computation.109 | convolution fusion | flops 59474800 | bytes 2320384 | tf_op jit(solution)/shard_map/sub | solution.py:86
  33.6 1.7 fusion.31
  36.8 1.4 fusion.4
  39.4 2.1 copy.35
  41.5 2.5 %concatenate.37 = f32[20,44,128]{2,1,0:T(8,128)} reshape(f32[880,2,64]{2,1,0:T(2,128)} %copy.35) | data formatting | bytes 901120 | tf_op jit(solution)/shard_map/concatenate | solution.py:119
  44.0 1.2 copy.38
  45.2 1.7 concatenate.40
  46.9 2.9 %fusion.66 = (f32[2,256]{1,0:T(2,128)S(1)}, f32[2,256,880]{1,2,0:T(8,128)}) fusion(pred[256,880]{0,1:T(8,128)(4,1)} %copy.22, bf16[256,2,64]{0,2,1:T(8,128)(2,1)} %bitcast.143, bf16[880,2,64]{0,2,1:T(8,128)(2,1)S(1)} %bitcast.118), kind=kOutput, calls=%fused_computation.110 | convolution fusion | flops 59474800 | bytes 2320384 | tf_op jit(solution)/shard_map/sub | solution.py:86
  49.9 1.7 fusion.32
  55.8 2.1 copy.36
  57.9 2.5 %concatenate.38 = f32[20,44,128]{2,1,0:T(8,128)} reshape(f32[880,2,64]{2,1,0:T(2,128)} %copy.36) | data formatting | bytes 901120 | tf_op jit(solution)/shard_map/concatenate | solution.py:119
  60.4 2.1 copy.39
  62.5 2.5 %concatenate.41 = f32[20,44,128]{2,1,0:T(8,128)} reshape(f32[880,2,64]{2,1,0:T(2,128)} %copy.39) | data formatting | bytes 901120 | tf_op jit(solution)/shard_map/concatenate | solution.py:119
  65.0 3.0 %fusion.64 = (f32[2,256]{1,0:T(2,128)S(1)}, f32[2,256,880]{1,2,0:T(8,128)}) fusion(pred[256,880]{0,1:T(8,128)(4,1)} %copy.22, bf16[256,2,64]{0,2,1:T(8,128)(2,1)S(1)} %bitcast.141, bf16[880,2,64]{0,2,1:T(8,128)(2,1)} %bitcast.120), kind=kOutput, calls=%fused_computation.108 | convolution fusion | flops 59474800 | bytes 2320384 | tf_op jit(solution)/shard_map/sub | solution.py:86
  68.0 1.7 fusion.30
  69.7 1.2 convolution_bitcast_fusion.3
  73.9 2.1 copy.34
  76.0 2.5 %concatenate.36 = f32[20,44,128]{2,1,0:T(8,128)} reshape(f32[880,2,64]{2,1,0:T(2,128)} %copy.34) | data formatting | bytes 901120 | tf_op jit(solution)/shard_map/concatenate | solution.py:119
  78.4 2.1 copy.37
  80.6 2.5 %concatenate.39 = f32[20,44,128]{2,1,0:T(8,128)} reshape(f32[880,2,64]{2,1,0:T(2,128)} %copy.37) | data formatting | bytes 901120 | tf_op jit(solution)/shard_map/concatenate | solution.py:119
  86.5 3.5 %collective-permute-start.4 = (f32[20,6,768]{2,1,0:T(8,128)S(1)}, f32[20,6,768]{2,1,0:T(8,128)S(1)}, u32[]{:S(2)}, u32[]{:S(2)}) collective-permute-start(f32[20,6,768]{2,1,0:T(8,128)S(1)} %get-tuple-element.55), channel_id=1, source_target_pairs={{0,8},{8,16},{16,24},{1,9},{9,17},{17,25},{2,10},{10,18},{18,26},{... | collective-permute-start | bytes 1105928 | tf_op jit(solution)/shard_map/ppermute | solution.py:18
  90.0 1.3 collective-permute-start.5
  91.3 1.5 slice.215
  92.8 3.5 %collective-permute-done.4 = f32[20,6,768]{2,1,0:T(8,128)S(1)} collective-permute-done((f32[20,6,768]{2,1,0:T(8,128)S(1)}, f32[20,6,768]{2,1,0:T(8,128)S(1)}, u32[]{:S(2)}, u32[]{:S(2)}) %collective-permute-start.4) | collective-permute-done | bytes 368672 | tf_op jit(solution)/shard_map/ppermute | solution.py:18
  96.4 3.8 %scatter-add.14 = f32[20,32,768]{2,1,0:T(8,128)} dynamic-update-slice(f32[20,32,768]{2,1,0:T(8,128)} %slice.215, f32[20,6,768]{2,1,0:T(8,128)S(1)} %slice_add_fusion.3, s32[]{:T(128)} %constant.134.clone.1, s32[]{:T(128)} %constant.134.clone.1, s32[]{:T(128)} %constant.134.clone.1) | dynamic-update-slice | bytes 737284 | tf_op jit(solution)/shard_map/scatter-add | solution.py:127
  101.0 1.2 slice_add_fusion.2
  102.3 3.0 %scatter-add.15 = f32[20,32,768]{2,1,0:T(8,128)} dynamic-update-slice(f32[20,32,768]{2,1,0:T(8,128)} %scatter-add.14, f32[20,6,768]{2,1,0:T(8,128)S(1)} %slice_add_fusion.2, s32[]{:T(128)} %constant.134.clone.1, s32[]{:T(128)} %constant.143.clone.1, s32[]{:T(128)} %constant.134.clone.1) | dynamic-update-slice | bytes 737284 | tf_op jit(solution)/shard_map/scatter-add | solution.py:128
  105.3 2.4 %fusion.58 = (f32[6,32,768]{2,1,0:T(8,128)}, f32[6,32,768]{2,1,0:T(8,128)}) fusion(f32[20,32,768]{2,1,0:T(8,128)} %scatter-add.15), kind=kLoop, calls=%fused_computation.102 | loop fusion | bytes 2359296 | tf_op jit(solution)/shard_map/slice | solution.py:129
  107.8 10.0 %collective-permute-start.6 = (f32[6,32,768]{2,1,0:T(8,128)}, f32[6,32,768]{2,1,0:T(8,128)}, u32[]{:S(2)}, u32[]{:S(2)}) collective-permute-start(f32[6,32,768]{2,1,0:T(8,128)} %get-tuple-element.57), channel_id=1, source_target_pairs={{0,1},{1,2},{2,3},{3,4},{4,5},{5,6},{6,7},{8,9},{9,10},{10,11},{11... | collective-permute-start | bytes 1769480 | tf_op jit(solution)/shard_map/ppermute | solution.py:18
  118.1 1.3 collective-permute-start.7
  119.9 1.4 fusion.15
  121.5 1.2 slice.220
  122.7 1.3 fusion.34
  124.0 2.7 %collective-permute-done.7 = f32[6,32,768]{2,1,0:T(8,128)S(1)} collective-permute-done((f32[6,32,768]{2,1,0:T(8,128)}, f32[6,32,768]{2,1,0:T(8,128)S(1)}, u32[]{:S(2)}, u32[]{:S(2)}) %collective-permute-start.7) | collective-permute-done | bytes 589856 | tf_op jit(solution)/shard_map/ppermute | solution.py:19
  126.9 1.5 convolution_convert_fusion.1
  128.4 2.4 %convolution_bitcast_fusion = f32[768,1152]{0,1:T(8,128)} fusion(bf16[256,768]{1,0:T(8,128)(2,1)S(1)} %bitcast.140, bf16[256,768]{1,0:T(8,128)(2,1)S(1)} %bitcast.117, bf16[256,128]{1,0:T(8,128)(2,1)S(1)} %copy.42, bf16[256,128]{1,0:T(8,128)(2,1)S(1)} %copy.41, bf16[256,128]{1,0:T(8,128)(2,1)S(1)} %copy.40), kind=kOutput, calls=%fused_computation.3 | convolution fusion | flops 455344128 | bytes 4521984 | tf_op jit(solution)/shard_map/dot_general | solution.py:142
  130.8 94.7 %all-reduce.1 = bf16[768,1152]{0,1:T(8,128)(2,1)S(1)} all-reduce(f32[768,1152]{0,1:T(8,128)} %convolution_bitcast_fusion), channel_id=1, replica_groups=mesh['ew'=4,'ns'=8] {'ew','ns'}, use_global_device_ids=true, to_apply=%region_9.10 | all-reduce | flops 884736 | bytes 5308416 | tf_op jit(solution)/shard_map/psum | solution.py:145
  225.5 2.2 copy.43
  (104 shorter events, 26.0 us)
Async XLA Ops:
  0.6 1.5 copy-start
  2.1 8.1 %copy-start.23 = (bf16[8,32,384]{2,1,0:T(8,128)(2,1)S(1)}, bf16[8,32,384]{2,1,0:T(8,128)(2,1)}, u32[]{:S(2)}) copy-start(bf16[8,32,384]{2,1,0:T(8,128)(2,1)} %param.13) | copy-start | bytes 589828
  3.9 12.5 %copy-start.1 = (bf16[256,768]{1,0:T(8,128)(2,1)}, bf16[256,768]{1,0:T(8,128)(2,1)S(1)}, u32[]{:S(2)}) copy-start(bf16[256,768]{1,0:T(8,128)(2,1)S(1)} %slice.198) | copy-start | bytes 1179652
  3.9 9.7 %collective-permute-start = (bf16[8,6,768]{2,1,0:T(8,128)(2,1)S(1)}, bf16[8,6,768]{2,1,0:T(8,128)(2,1)S(1)}, u32[]{:S(2)}, u32[]{:S(2)}) collective-permute-start(bf16[8,6,768]{2,1,0:T(8,128)(2,1)S(1)} %get-tuple-element.69), channel_id=1, source_target_pairs={{0,8},{8,16},{16,24},{1,9},{9,17},{17,25},{2,10},{10,18},{18,26},{... | collective-permute-start | bytes 221192 | tf_op jit(solution)/shard_map/ppermute | solution.py:18
  8.9 6.5 %collective-permute-start.1 = (bf16[8,6,768]{2,1,0:T(8,128)(2,1)S(1)}, bf16[8,6,768]{2,1,0:T(8,128)(2,1)S(1)}, u32[]{:S(2)}, u32[]{:S(2)}) collective-permute-start(bf16[8,6,768]{2,1,0:T(8,128)(2,1)S(1)} %get-tuple-element.70), channel_id=1, source_target_pairs={{8,0},{16,8},{24,16},{9,1},{17,9},{25,17},{10,2},{18,10},{26,18},{... | collective-permute-start | bytes 221192 | tf_op jit(solution)/shard_map/ppermute | solution.py:19
  15.4 4.3 %copy-start.18 = (bf16[8,6,768]{2,1,0:T(8,128)(2,1)}, bf16[8,6,768]{2,1,0:T(8,128)(2,1)S(1)}, u32[]{:S(2)}) copy-start(bf16[8,6,768]{2,1,0:T(8,128)(2,1)S(1)} %collective-permute-done.1) | copy-start | bytes 221188
  16.4 5.9 %collective-permute-start.2 = (bf16[6,44,768]{2,1,0:T(8,128)(2,1)}, bf16[6,44,768]{2,1,0:T(8,128)(2,1)}, u32[]{:S(2)}, u32[]{:S(2)}) collective-permute-start(bf16[6,44,768]{2,1,0:T(8,128)(2,1)} %get-tuple-element.67), channel_id=1, source_target_pairs={{0,1},{1,2},{2,3},{3,4},{4,5},{5,6},{6,7},{8,9},{9,10},{10,11},{11... | collective-permute-start | bytes 1216520 | tf_op jit(solution)/shard_map/ppermute | solution.py:18
  18.4 4.8 %collective-permute-start.3 = (bf16[6,44,768]{2,1,0:T(8,128)(2,1)S(1)}, bf16[6,44,768]{2,1,0:T(8,128)(2,1)}, u32[]{:S(2)}, u32[]{:S(2)}) collective-permute-start(bf16[6,44,768]{2,1,0:T(8,128)(2,1)S(1)} %get-tuple-element.68), channel_id=1, source_target_pairs={{1,0},{2,1},{3,2},{4,3},{5,4},{6,5},{7,6},{9,8},{10,9},{11,10},{12... | collective-permute-start | bytes 1216520 | tf_op jit(solution)/shard_map/ppermute | solution.py:19
  28.0 7.7 %copy-start.16 = (bf16[880,128]{0,1:T(8,128)(2,1)}, bf16[880,128]{0,1:T(8,128)(2,1)S(1)}, u32[]{:S(2)}) copy-start(bf16[880,128]{0,1:T(8,128)(2,1)S(1)} %copy.48) | copy-start | bytes 675844
  28.2 5.4 %copy-start.12 = (bf16[880,128]{0,1:T(8,128)(2,1)}, bf16[880,128]{0,1:T(8,128)(2,1)S(1)}, u32[]{:S(2)}) copy-start(bf16[880,128]{0,1:T(8,128)(2,1)S(1)} %copy.47) | copy-start | bytes 675844
  33.6 1.7 copy-start.17
  35.3 1.5 copy-start.9
  36.8 1.4 copy-start.22
  49.9 2.8 %copy-start.15 = (bf16[880,128]{0,1:T(8,128)(2,1)S(1)}, bf16[880,128]{0,1:T(8,128)(2,1)}, u32[]{:S(2)}) copy-start(bf16[880,128]{0,1:T(8,128)(2,1)} %copy.51) | copy-start | bytes 675844
  51.5 1.7 copy-start.10
  53.2 1.4 copy-start.21
  53.7 0.9 copy-start.2
  57.9 7.1 %copy-start.20 = (bf16[256,128]{0,1:T(8,128)(2,1)S(1)}, bf16[256,128]{0,1:T(8,128)(2,1)}, u32[]{:S(2)}) copy-start(bf16[256,128]{0,1:T(8,128)(2,1)} %copy.23) | copy-start | bytes 196612
  68.0 2.9 %copy-start.14 = (bf16[880,128]{0,1:T(8,128)(2,1)S(1)}, bf16[880,128]{0,1:T(8,128)(2,1)}, u32[]{:S(2)}) copy-start(bf16[880,128]{0,1:T(8,128)(2,1)} %copy.45) | copy-start | bytes 675844
  69.7 1.7 copy-start.8
  71.8 0.9 copy-start.4
  83.0 2.3 %copy-start.6 = (f32[20,44,128]{2,1,0:T(8,128)S(1)}, f32[20,44,128]{2,1,0:T(8,128)}, u32[]{:S(2)}) copy-start(f32[20,44,128]{2,1,0:T(8,128)} %concatenate.38) | copy-start | bytes 1351684
  83.0 2.4 %copy-start.7 = (f32[20,44,128]{2,1,0:T(8,128)S(1)}, f32[20,44,128]{2,1,0:T(8,128)}, u32[]{:S(2)}) copy-start(f32[20,44,128]{2,1,0:T(8,128)} %concatenate.39) | copy-start | bytes 1351684
  84.2 1.3 copy-start.5
  86.5 9.8 %collective-permute-start.4 = (f32[20,6,768]{2,1,0:T(8,128)S(1)}, f32[20,6,768]{2,1,0:T(8,128)S(1)}, u32[]{:S(2)}, u32[]{:S(2)}) collective-permute-start(f32[20,6,768]{2,1,0:T(8,128)S(1)} %get-tuple-element.55), channel_id=1, source_target_pairs={{0,8},{8,16},{16,24},{1,9},{9,17},{17,25},{2,10},{10,18},{18,26},{... | collective-permute-start | bytes 1105928 | tf_op jit(solution)/shard_map/ppermute | solution.py:18
  90.0 11.0 %collective-permute-start.5 = (f32[20,6,768]{2,1,0:T(8,128)}, f32[20,6,768]{2,1,0:T(8,128)}, u32[]{:S(2)}, u32[]{:S(2)}) collective-permute-start(f32[20,6,768]{2,1,0:T(8,128)} %get-tuple-element.54), channel_id=1, source_target_pairs={{8,0},{16,8},{24,16},{9,1},{17,9},{25,17},{10,2},{18,10},{26,18},{... | collective-permute-start | bytes 1105928 | tf_op jit(solution)/shard_map/ppermute | solution.py:19
  105.3 12.5 %copy-start.13 = (bf16[880,128]{0,1:T(8,128)(2,1)S(1)}, bf16[880,128]{0,1:T(8,128)(2,1)}, u32[]{:S(2)}) copy-start(bf16[880,128]{0,1:T(8,128)(2,1)} %copy-done.12) | copy-start | bytes 675844
  105.3 14.1 %copy-start.3 = (bf16[2,256,880]{1,2,0:T(8,128)(2,1)S(1)}, bf16[2,256,880]{1,2,0:T(8,128)(2,1)}, u32[]{:S(2)}) copy-start(bf16[2,256,880]{1,2,0:T(8,128)(2,1)} %copy-done.2) | copy-start | bytes 2703364
  107.8 12.2 %copy-start.11 = (bf16[880,128]{0,1:T(8,128)(2,1)S(1)}, bf16[880,128]{0,1:T(8,128)(2,1)}, u32[]{:S(2)}) copy-start(bf16[880,128]{0,1:T(8,128)(2,1)} %copy.44) | copy-start | bytes 675844
  107.8 14.9 %collective-permute-start.6 = (f32[6,32,768]{2,1,0:T(8,128)}, f32[6,32,768]{2,1,0:T(8,128)}, u32[]{:S(2)}, u32[]{:S(2)}) collective-permute-start(f32[6,32,768]{2,1,0:T(8,128)} %get-tuple-element.57), channel_id=1, source_target_pairs={{0,1},{1,2},{2,3},{3,4},{4,5},{5,6},{6,7},{8,9},{9,10},{10,11},{11... | collective-permute-start | bytes 1769480 | tf_op jit(solution)/shard_map/ppermute | solution.py:18
  118.1 8.7 %collective-permute-start.7 = (f32[6,32,768]{2,1,0:T(8,128)}, f32[6,32,768]{2,1,0:T(8,128)S(1)}, u32[]{:S(2)}, u32[]{:S(2)}) collective-permute-start(f32[6,32,768]{2,1,0:T(8,128)} %get-tuple-element.56), channel_id=1, source_target_pairs={{1,0},{2,1},{3,2},{4,3},{5,4},{6,5},{7,6},{9,8},{10,9},{11,10},{12... | collective-permute-start | bytes 1769480 | tf_op jit(solution)/shard_map/ppermute | solution.py:19
  126.9 1.5 copy-start.19
where the time goes:
time: 229 us; the launch traced here: 228 us
  blocking collectives  94.7 us (41%)
  local copies, waits for them, and re-layouts  60.3 us (26%)
  matrix products  25.9 us (11%)
  starting transfers between devices  25.7 us (11%)
  other arithmetic  10.1 us (4%)
  waiting for transfers between devices  9.82 us (4%)
    psum x1, blocking collectives, local(): grad_w = lax.psum(weight_part, ('ew', 'ns')).astype(jnp.bfloat16)  94.7 us
    ppermute x4, starting transfers between devices, padded(): before = lax.ppermute(last, axis, up)  20.5 us
    concatenate x7, local copies, waits for them, and re-layouts, local(): jnp.concatenate(key_parts + value_parts, axis=1)  14.2 us
    unnamed x63, local copies, waits for them, and re-layouts  13.1 us
    sub x3, matrix products, local(): exp_scores = jnp.exp(scores - row_max)  8.88 us
    mul x3, local copies, waits for them, and re-layouts, local(): jnp.einsum('hqk,qhd->khd', score_grad, query_pair, preferred_element_type...  6.33 us
    ppermute x4, waiting for transfers between devices, padded(): after = lax.ppermute(leading, axis, down)  6.31 us
    transpose x3, local copies, waits for them, and re-layouts, local(): jnp.einsum('hqk,qhd->khd', probs_low, grad_pair, preferred_element_type=j...  5.47 us
  transfers between devices with their start and end apart: 8, of which 5 were waited for; matrix products, arithmetic and copies ran while one was open for 7% of the time, Pallas kernels for 0%

commit v1 on v0

v1 whole, which is shorter than its diff:
```python
import functools

import jax
import jax.numpy as jnp
from jax import lax
from jax.experimental import pallas as pl
from jax.experimental.pallas import tpu as pltpu
from jax.sharding import PartitionSpec as P

HEADS = 6
HDIM = 64
RADIUS = 6
MESH = pl.DeviceIdType.MESH


def padded(value, sides, width):
    for axis, dim in sides:
        size, length = (lax.axis_size(axis), value.shape[dim])
        up = [(i, (i + 1) % size) for i in range(size - 1)]
        down = [(j, i) for i, j in up]
        last = lax.slice_in_dim(value, length - width, length, axis=dim)
        leading = lax.slice_in_dim(value, 0, width, axis=dim)
        before = lax.ppermute(last, axis, up)
        after = lax.ppermute(leading, axis, down)
        value = jnp.concatenate([before, value, after], axis=dim)
    return value


def attention_kernel(nb, qr, qc, kr, kc, q_ref, k_ref, v_ref, g_ref, dq_ref, dk_ref, dv_ref):
    count = q_ref.shape[0] // nb
    span = kr.shape[2]
    step = (k_ref.shape[0] - span) // max(nb - 1, 1)
    dk_ref[...] = jnp.zeros_like(dk_ref)
    dv_ref[...] = jnp.zeros_like(dv_ref)
    for b in range(nb):
        rows = pl.ds(b * count, count)
        keys = pl.ds(b * step, span)
        ok = (jnp.abs(qr[rows, :] - kr[b]) <= RADIUS) & (jnp.abs(qc[rows, :] - kc[b]) <= RADIUS)
        bias = jnp.where(ok, 0.0, -1e30)
        q8 = q_ref[rows, :] * jnp.bfloat16(HDIM ** -0.5)
        kb, vb, g = k_ref[keys, :], v_ref[keys, :], g_ref[rows, :]
        dqs, dks, dvs = [], [], []
        for h in range(2):
            cols = slice(h * HDIM, (h + 1) * HDIM)
            qh, kh, vh, gh = q8[:, cols], kb[:, cols], vb[:, cols], g[:, cols]
            nt = (((1,), (1,)), ((), ()))
            tn = (((0,), (0,)), ((), ()))
            dot = functools.partial(lax.dot_general, preferred_element_type=jnp.float32)
            s = dot(qh, kh, nt) + bias
            e = jnp.exp(s - jnp.max(s, axis=1, keepdims=True))
            p = e * (1.0 / jnp.sum(e, axis=1, keepdims=True))
            pb = p.astype(jnp.bfloat16)
            att = jnp.dot(pb, vh, preferred_element_type=jnp.float32)
            delta = jnp.sum(gh.astype(jnp.float32) * att, axis=1, keepdims=True)
            dp = dot(gh, vh, nt)
            ds = (p * (dp - delta)).astype(jnp.bfloat16)
            dqs.append(jnp.dot(ds, kh, preferred_element_type=jnp.float32) * (HDIM ** -0.5))
            dks.append(dot(ds, qh, tn))
            dvs.append(dot(pb, gh, tn))
        dq_ref[rows, :] = jnp.concatenate(dqs, axis=1)
        dk_ref[keys, :] += jnp.concatenate(dks, axis=1)
        dv_ref[keys, :] += jnp.concatenate(dvs, axis=1)


def attention(q, kv, g, qr, qc, kr, kc, nb):
    count, width = q.shape
    extent = kv.shape[0]
    lanes = 2 * HDIM
    groups = width // lanes
    whole = lambda a: pl.BlockSpec(a.shape, lambda i: (0,) * a.ndim)
    qs = pl.BlockSpec((count, lanes), lambda i: (0, i))
    ks = pl.BlockSpec((extent, lanes), lambda i: (0, i))
    vs = pl.BlockSpec((extent, lanes), lambda i: (0, i + groups))
    return pl.pallas_call(
        functools.partial(attention_kernel, nb),
        grid=(groups,),
        in_specs=[whole(qr), whole(qc), whole(kr), whole(kc), qs, ks, vs, qs],
        out_specs=[qs, ks, ks],
        out_shape=[
            jax.ShapeDtypeStruct((count, width), jnp.float32),
            jax.ShapeDtypeStruct((extent, width), jnp.float32),
            jax.ShapeDtypeStruct((extent, width), jnp.float32),
        ],
        compiler_params=pltpu.CompilerParams(vmem_limit_bytes=40 << 20),
        cost_estimate=pl.CostEstimate(
            flops=14 * count * extent * width, bytes_accessed=8 << 20, transcendentals=count * extent * HEADS
        ),
    )(qr, qc, kr, kc, q, kv, kv, g)


CH = 128


def weight_kernel(
    nn, ne, tok_ref, dq_ref, out_ref, recv, part, slots,
    a_send, a_recv, r_send, r_recv, z_send, z_recv, p_send, p_recv, f_send, f_recv,
):
    e, n = lax.axis_index("ew"), lax.axis_index("ns")
    share = recv.shape[1]
    count = tok_ref.shape[0] // nn
    chunks = part.shape[0]
    owner = [min((c + 1) // 2, ne - 1) for c in range(chunks)]
    slot_of = [sum(1 for d in range(c) if owner[d] == owner[c]) for c in range(chunks)]
    core = lax.rem(n, 2)
    sibling = n + 1 - 2 * core

    def rows_of(d):
        return pl.ds(pl.multiple_of(d * share, 16), share)

    def at(d, m):
        return (d, m)

    barrier = pltpu.get_barrier_semaphore()
    for k in range(1, nn):
        pl.semaphore_signal(barrier, inc=1, device_id=at(e, lax.rem(n + k, nn)), device_id_type=MESH)
    for k in range(1, ne):
        pl.semaphore_signal(barrier, inc=1, device_id=at(lax.rem(e + k, ne), n), device_id_type=MESH)
    pl.semaphore_wait(barrier, nn - 1 + ne - 1)

    def exchange(k):
        to = lax.rem(n + k, nn)
        return pltpu.make_async_remote_copy(
            src_ref=dq_ref.at[rows_of(to)], dst_ref=recv.at[n],
            send_sem=a_send.at[k], recv_sem=a_recv.at[n],
            device_id=at(e, to), device_id_type=MESH,
        )

    def arrived(k):
        src = lax.rem(n + nn - k, nn)
        return pltpu.make_async_remote_copy(
            src_ref=recv.at[src], dst_ref=recv.at[src],
            send_sem=a_send.at[k], recv_sem=a_recv.at[src],
            device_id=at(e, src), device_id_type=MESH,
        )

    for k in range(1, nn):
        exchange(k).start()
    recv[n] = dq_ref[rows_of(n), :]
    for k in range(1, nn):
        arrived(k).wait_recv()

    def reduce_copy(c, src):
        return pltpu.make_async_remote_copy(
            src_ref=part.at[c], dst_ref=slots.at[slot_of[c], src],
            send_sem=r_send.at[c], recv_sem=r_recv.at[slot_of[c], src],
            device_id=at(owner[c], n), device_id_type=MESH,
        )

    order = [c for c in range(chunks)]
    for c in order:
        total = jnp.zeros((share, CH), jnp.float32)
        for s in range(nn):
            total += jnp.dot(
                recv[s], tok_ref[s * count : (s + 1) * count, c * CH : (c + 1) * CH],
                preferred_element_type=jnp.float32,
            )
        part[c] = total

        @pl.when(e != owner[c])
        def _():
            reduce_copy(c, e).start()

    def spot(c, m):
        return out_ref.at[rows_of(m), c * CH : (c + 1) * CH]

    def column_copy(c, k):
        return pltpu.make_async_remote_copy(
            src_ref=spot(c, n), dst_ref=spot(c, n),
            send_sem=z_send.at[c, k], recv_sem=z_recv.at[c],
            device_id=at(lax.rem(owner[c] + k, ne), n), device_id_type=MESH,
        )

    def plane_copy(c, m, to, sem, k, rsem):
        return pltpu.make_async_remote_copy(
            src_ref=spot(c, m), dst_ref=spot(c, m),
            send_sem=sem.at[c, k], recv_sem=rsem.at[c, m],
            device_id=at(e, to), device_id_type=MESH,
        )

    def peers(k):
        return lax.rem(n + 2 * k, nn)

    def spread(c):
        for k in range(1, nn // 2):
            plane_copy(c, n, peers(k), p_send, k, p_recv).start()
        plane_copy(c, n, sibling, p_send, 0, p_recv).start()

    for c in order:

        @pl.when(e == owner[c])
        def _():
            total = part[c]
            for k in range(1, ne):
                src = (owner[c] + k) % ne
                reduce_copy(c, src).wait_recv()
                total += slots[slot_of[c], src]
            out_ref[rows_of(n), c * CH : (c + 1) * CH] = total.astype(jnp.bfloat16)
            for k in range(1, ne):
                column_copy(c, k).start()
            spread(c)

    for c in order:

        @pl.when(e != owner[c])
        def _():
            column_copy(c, 1).wait_recv()
            spread(c)

    for c in order:
        for k in range(1, nn // 2):
            m = peers(k)
            plane_copy(c, m, sibling, p_send, 0, p_recv).wait_recv()
            plane_copy(c, m, sibling, f_send, k, f_recv).start()

    for c in order:
        plane_copy(c, sibling, sibling, p_send, 0, p_recv).wait_recv()
        for k in range(1, nn // 2):
            m = lax.rem(sibling + 2 * k, nn)
            plane_copy(c, m, sibling, f_send, k, f_recv).wait_recv()

    for k in range(1, nn):
        exchange(k).wait_send()
    for c in order:

        @pl.when(e != owner[c])
        def _():
            reduce_copy(c, e).wait_send()

        @pl.when(e == owner[c])
        def _():
            for k in range(1, ne):
                column_copy(c, k).wait_send()

        for k in range(nn // 2):
            plane_copy(c, n, sibling, p_send, k, p_recv).wait_send()
        for k in range(1, nn // 2):
            plane_copy(c, n, sibling, f_send, k, f_recv).wait_send()


def weight_sum(tok_all, dqkv_t, nn, ne):
    wide, count = dqkv_t.shape
    features = tok_all.shape[1]
    share, chunks = wide // nn, features // CH
    dma = pltpu.SemaphoreType.DMA
    vm = pl.BlockSpec(memory_space=pltpu.VMEM)
    return pl.pallas_call(
        functools.partial(weight_kernel, nn, ne),
        out_shape=jax.ShapeDtypeStruct((wide, features), jnp.bfloat16),
        in_specs=[vm, vm],
        out_specs=vm,
        scratch_shapes=[
            pltpu.VMEM((nn, share, count), jnp.bfloat16),
            pltpu.VMEM((chunks, share, CH), jnp.float32),
            pltpu.VMEM((2, ne, share, CH), jnp.float32),
            dma((nn,)), dma((nn,)),
            dma((chunks,)), dma((2, ne)),
            dma((chunks, ne)), dma((chunks,)),
            dma((chunks, nn // 2)), dma((chunks, nn)),
            dma((chunks, nn // 2)), dma((chunks, nn)),
        ],
        compiler_params=pltpu.CompilerParams(
            collective_id=1, has_side_effects=True, vmem_limit_bytes=40 << 20
        ),
        cost_estimate=pl.CostEstimate(
            flops=2 * share * nn * count * features, bytes_accessed=8 << 20, transcendentals=0
        ),
    )(tok_all, dqkv_t)


def local(tokens, w_qkv, grad_out):
    tile_rows, tile_cols, features = tokens.shape
    nn, ne = lax.axis_size("ns"), lax.axis_size("ew")
    width = w_qkv.shape[1] // 3
    count = tile_rows * tile_cols
    flat_tokens = tokens.reshape(count, features)
    paired = nn == 8 and ne == 4
    if paired:
        tok_all = lax.all_gather(flat_tokens, "ns", axis=0, tiled=True)
    projected = jnp.dot(flat_tokens, w_qkv, preferred_element_type=jnp.float32).astype(jnp.bfloat16)
    wide_kv = padded(
        projected[:, width:].reshape(tile_rows, tile_cols, 2 * width),
        (("ew", 1), ("ns", 0)),
        RADIUS,
    )
    ext_rows, ext_cols = (wide_kv.shape[0], wide_kv.shape[1])
    key_values = wide_kv.reshape(ext_rows * ext_cols, 2 * width)
    nb = 2
    row0 = lax.axis_index("ns") * tile_rows
    col0 = lax.axis_index("ew") * tile_cols
    qi = jnp.arange(count, dtype=jnp.int32)
    qr = (row0 + qi // tile_cols)[:, None]
    qc = (col0 + qi % tile_cols)[:, None]
    ki = jnp.arange(ext_rows * ext_cols, dtype=jnp.int32)
    kr = row0 - RADIUS + ki // ext_cols
    kc = col0 - RADIUS + ki % ext_cols
    inside = (kr >= 0) & (kr < nn * tile_rows) & (kc >= 0) & (kc < ne * tile_cols)
    kr = jnp.where(inside, kr, -1000)
    per = tile_rows // nb
    span = (per + 2 * RADIUS) * ext_cols
    pick = lambda a: jnp.stack([a[b * per * ext_cols :][:span][None] for b in range(nb)])
    query_grad, key_grad, value_grad = attention(
        projected[:, :width], key_values, grad_out.reshape(count, width), qr, qc, pick(kr), pick(kc), nb
    )
    ext_grads = jnp.concatenate([key_grad, value_grad], axis=1).reshape(ext_rows, ext_cols, 2 * width)
    side_strips = jnp.concatenate([ext_grads[:, :RADIUS], ext_grads[:, tile_cols + RADIUS :]], axis=1)
    from_sides = padded(side_strips, (("ew", 1),), RADIUS)
    middle = ext_grads[:, RADIUS : tile_cols + RADIUS]
    middle = middle + jnp.pad(from_sides[:, :RADIUS], ((0, 0), (0, tile_cols - RADIUS), (0, 0)))
    middle = middle + jnp.pad(from_sides[:, 3 * RADIUS :], ((0, 0), (tile_cols - RADIUS, 0), (0, 0)))
    edge_strips = jnp.concatenate([middle[:RADIUS], middle[tile_rows + RADIUS :]], axis=0)
    from_edges = padded(edge_strips, (("ns", 0),), RADIUS)
    owned = middle[RADIUS : tile_rows + RADIUS]
    owned = owned + jnp.pad(from_edges[:RADIUS], ((0, tile_rows - RADIUS), (0, 0), (0, 0)))
    owned = owned + jnp.pad(from_edges[3 * RADIUS :], ((tile_rows - RADIUS, 0), (0, 0), (0, 0)))
    dqkv = jnp.concatenate([query_grad, owned.reshape(count, 2 * width)], axis=1).astype(
        jnp.bfloat16
    )
    grad_tokens = (
        jnp.dot(dqkv, w_qkv.T, preferred_element_type=jnp.float32)
        .astype(jnp.bfloat16)
        .reshape(tile_rows, tile_cols, features)
    )
    if paired:
        grad_w = weight_sum(tok_all, dqkv.T, nn, ne).T
    else:
        weight_part = lax.dot_general(
            flat_tokens, dqkv, (((0,), (0,)), ((), ())), preferred_element_type=jnp.float32
        )
        grad_w = lax.psum(weight_part, ("ew", "ns")).astype(jnp.bfloat16)
    return (grad_tokens, grad_w)


def solution(mesh):
    in_specs = (P("ns", "ew", None), P(), P("ns", "ew", None))
    out_specs = (P("ns", "ew", None), P())
    return jax.shard_map(local, mesh=mesh, in_specs=in_specs, out_specs=out_specs, check_vma=False)
```

time: 229 us -> 161 us (0.70)
  blocking collectives: 94.7 us -> 0 us
  Pallas kernels: 0 us -> 57.4 us
  local copies, waits for them, and re-layouts: 60.3 us -> 20.7 us
  matrix products: 25.9 us -> 3.15 us
  waiting for transfers between devices: 9.82 us -> 25.6 us
  between operations: 1.2 us -> 14.3 us
  starting transfers between devices: 25.7 us -> 28.8 us
    psum x1 -> x0, blocking collectives: 94.7 us -> none  [local(): grad_w = lax.psum(weight_part, ('ew', 'ns')).astype(jnp.bfloat16)]
    pallas_call x0 -> x2, Pallas kernels: none -> 57.4 us  [the longest x1 44.6 us: weight_sum(): pl.pallas_call(functools.partial(weight_kernel, nn, ne), out_shape=jax.Sh...]
    concatenate x7 -> x0, local copies, waits for them, and re-layouts: 14.2 us -> none  [local(): jnp.concatenate(key_parts + value_parts, axis=1)]
    dot_general x16 -> x0, matrix products: 13.8 us -> none  [the longest x3 3.46 us: local(): jnp.einsum('hqk,qhd->khd', score_grad, query_pair, preferred_element_type...]
    ppermute x4, waiting for transfers between devices: 6.31 us -> 18.7 us  [padded(): after = lax.ppermute(leading, axis, down)]
    sub x3 -> x0, matrix products: 8.88 us -> none  [local(): exp_scores = jnp.exp(scores - row_max)]
    scatter-add x2 -> x0, local copies, waits for them, and re-layouts: 6.83 us -> none  [the longest x1 3.8 us: local(): middle = middle.at[:, :RADIUS].add(from_sides[:, :RADIUS])]
    slice x10 -> x5, local copies, waits for them, and re-layouts: 9.81 us -> 3.37 us  [the longest x1 1.41 us: local(): ext_grads[:, tile_cols + RADIUS:]]
  transfers between devices with their start and end apart: 8 -> 9, of which waited for: 5 -> 7; matrix products, arithmetic and copies ran while one was open for 7% -> 13% of each run, Pallas kernels for 0% -> 8%
where the time goes in v1:
time: 161 us; the launch traced here: 158 us
  Pallas kernels  57.4 us (36%)
  starting transfers between devices  28.8 us (18%)
  waiting for transfers between devices  25.6 us (16%)
  local copies, waits for them, and re-layouts  20.7 us (13%)
  between operations  14.3 us (9%)
  other arithmetic  8.37 us (5%)
  matrix products  3.15 us (2%)
    pallas_call x1, Pallas kernels, weight_sum(): pl.pallas_call(functools.partial(weight_kernel, nn, ne), out_shape=jax.Sh...  44.6 us
    ppermute x4, starting transfers between devices, padded(): before = lax.ppermute(last, axis, up)  23.6 us
    ppermute x4, waiting for transfers between devices, padded(): after = lax.ppermute(leading, axis, down)  18.7 us
    pallas_call x1, Pallas kernels, attention(): pl.pallas_call(functools.partial(attention_kernel, nb), grid=(groups,), i...  12.8 us
    unnamed x17, local copies, waits for them, and re-layouts  11 us
    ppermute x4, waiting for transfers between devices, padded(): before = lax.ppermute(last, axis, up)  6.14 us
    ppermute x4, starting transfers between devices, padded(): after = lax.ppermute(leading, axis, down)  5.17 us
    reshape x1, local copies, waits for them, and re-layouts, local(): jnp.concatenate([key_grad, value_grad], axis=1)  3.75 us
  transfers between devices with their start and end apart: 9, of which 7 were waited for; matrix products, arithmetic and copies ran while one was open for 13% of the time, Pallas kernels for 8%

profile of v1, /device:TPU:0, one launch (start us, length us, event | category | flops | bytes accessed | tf_op | source)
XLA Modules:
  0.0 158.2 jit_solution(2899081628058620007)
XLA Ops:
  7.2 0.0 copy-start
  7.2 0.0 all-gather.2.cloned.1.call-start
  7.2 0.7 all-gather.2.cloned.1.call-update
  7.9 0.7 copy-done
  8.6 1.7 %convolution_convert_fusion = bf16[256,1152]{1,0:T(8,128)(2,1)S(1)} fusion(bf16[256,768]{1,0:T(8,128)(2,1)} %bitcast.18, bf16[768,1152]{1,0:T(8,128)(2,1)S(1)} %copy-done), kind=kOutput, calls=%fused_computation.1 | convolution fusion | flops 453279744 | bytes 2752512 | tf_op jit(solution)/shard_map/dot_general | solution.py:279
  10.4 4.9 %collective-permute-start = (bf16[8,6,768]{2,1,0:T(8,128)(2,1)S(1)}, bf16[8,6,768]{2,1,0:T(8,128)(2,1)S(1)}, u32[]{:S(2)}, u32[]{:S(2)}) collective-permute-start(bf16[8,6,768]{2,1,0:T(8,128)(2,1)S(1)} %get-tuple-element.18), channel_id=1, source_target_pairs={{0,8},{8,16},{16,24},{1,9},{9,17},{17,25},{2,10},{10,18},{18,26},{... | collective-permute-start | bytes 221192 | tf_op jit(solution)/shard_map/ppermute | solution.py:23
  15.3 1.3 collective-permute-start.1
  16.7 0.1 fusion.28
  16.7 0.8 collective-permute-done
  17.5 4.3 %collective-permute-done.1 = bf16[8,6,768]{2,1,0:T(8,128)(2,1)S(1)} collective-permute-done((bf16[8,6,768]{2,1,0:T(8,128)(2,1)S(1)}, bf16[8,6,768]{2,1,0:T(8,128)(2,1)S(1)}, u32[]{:S(2)}, u32[]{:S(2)}) %collective-permute-start.1) | collective-permute-done | bytes 73760 | tf_op jit(solution)/shard_map/ppermute | solution.py:24
  21.9 0.2 pad_maximum_fusion.2
  22.0 0.1 fusion.25
  22.1 1.3 collective-permute-start.2
  23.4 1.3 collective-permute-start.3
  24.7 0.1 fusion.27
  24.8 0.7 slice.64.q_ref
  25.6 0.8 fusion.10
  26.3 2.5 %collective-permute-done.3 = bf16[6,44,768]{2,1,0:T(8,128)(2,1)S(1)} collective-permute-done((bf16[6,44,768]{2,1,0:T(8,128)(2,1)S(1)}, bf16[6,44,768]{2,1,0:T(8,128)(2,1)S(1)}, u32[]{:S(2)}, u32[]{:S(2)}) %collective-permute-start.3) | collective-permute-done | bytes 405536 | tf_op jit(solution)/shard_map/ppermute | solution.py:24
  28.8 1.3 pad_maximum_fusion.1
  30.2 2.2 %reshape.84.k_ref.v_ref = bf16[880,768]{1,0:T(8,128)(2,1)S(1)} reshape(bf16[20,44,768]{2,1,0:T(8,128)(2,1)} %pad_maximum_fusion.1) | data formatting | bytes 2703360 | tf_op jit(solution)/shard_map/reshape | solution.py:286
  32.4 1.0 copy-done.3
  33.4 0.9 copy-done.4
  34.3 0.9 copy-done.5
  35.2 0.9 copy-done.6
  36.1 12.8 %shard_map.50 = (f32[256,384]{1,0:T(8,128)S(1)}, f32[880,384]{1,0:T(8,128)S(1)}, f32[880,384]{1,0:T(8,128)S(1)}) custom-call(s32[256,1]{1,0:T(8,128)S(1)} %copy-done.4, s32[256,1]{1,0:T(8,128)S(1)} %copy-done.5, s32[2,1,704]{2,1,0:T(1,128)S(1)} %pad_add_fusion.kr, s32[2,1,704]{2,1,0:T(1,128)S(1)} %pad_add_fusion.1.kc, bf16[256,384]{1,0:T(8,128)(2,1)S(1)} %copy-done.3, ...), custom_call_target="tpu_custom_call" | custom-call | flops 1211105280 | bytes 8388608 | tf_op jit(solution)/shard_map/pallas_call | solution.py:74
  48.9 1.8 %pad_maximum_fusion = f32[880,768]{1,0:T(8,128)} fusion(f32[880,384]{1,0:T(8,128)S(1)} %get-tuple-element.7, f32[880,384]{1,0:T(8,128)S(1)} %get-tuple-element.6), kind=kLoop, calls=%fused_computation | loop fusion | flops 675840 | bytes 5406720 | tf_op jit(solution)/shard_map/concatenate | solution.py:304
  50.7 3.7 %reshape.86 = f32[20,44,768]{2,1,0:T(8,128)} reshape(f32[880,768]{1,0:T(8,128)} %pad_maximum_fusion) | data formatting | bytes 5406720 | tf_op jit(solution)/shard_map/reshape | solution.py:304
  54.4 1.4 fusion.23
  55.9 3.4 %collective-permute-start.4 = (f32[20,6,768]{2,1,0:T(8,128)S(1)}, f32[20,6,768]{2,1,0:T(8,128)S(1)}, u32[]{:S(2)}, u32[]{:S(2)}) collective-permute-start(f32[20,6,768]{2,1,0:T(8,128)S(1)} %get-tuple-element.12), channel_id=1, source_target_pairs={{0,8},{8,16},{16,24},{1,9},{9,17},{17,25},{2,10},{10,18},{18,26},{... | collective-permute-start | bytes 1105928 | tf_op jit(solution)/shard_map/ppermute | solution.py:23
  59.3 1.3 collective-permute-start.5
  60.6 5.0 %collective-permute-done.4 = f32[20,6,768]{2,1,0:T(8,128)S(1)} collective-permute-done((f32[20,6,768]{2,1,0:T(8,128)S(1)}, f32[20,6,768]{2,1,0:T(8,128)S(1)}, u32[]{:S(2)}, u32[]{:S(2)}) %collective-permute-start.4) | collective-permute-done | bytes 368672 | tf_op jit(solution)/shard_map/ppermute | solution.py:23
  65.6 4.4 %collective-permute-done.5 = f32[20,6,768]{2,1,0:T(8,128)S(1)} collective-permute-done((f32[20,6,768]{2,1,0:T(8,128)S(1)}, f32[20,6,768]{2,1,0:T(8,128)S(1)}, u32[]{:S(2)}, u32[]{:S(2)}) %collective-permute-start.5) | collective-permute-done | bytes 368672 | tf_op jit(solution)/shard_map/ppermute | solution.py:24
  70.0 2.0 %fusion = f32[20,32,768]{2,1,0:T(8,128)S(1)} fusion(f32[20,44,768]{2,1,0:T(8,128)} %reshape.86, f32[20,6,768]{2,1,0:T(8,128)S(1)} %collective-permute-done.5, f32[20,6,768]{2,1,0:T(8,128)S(1)} %collective-permute-done.4), kind=kLoop, calls=%fused_computation.3 | loop fusion | flops 983040 | bytes 4669440 | tf_op jit(solution)/shard_map/add | solution.py:309
  72.1 1.3 copy-done.7
  73.4 1.1 fusion.24
  74.5 13.9 %collective-permute-start.6 = (f32[6,32,768]{2,1,0:T(8,128)}, f32[6,32,768]{2,1,0:T(8,128)S(1)}, u32[]{:S(2)}, u32[]{:S(2)}) collective-permute-start(f32[6,32,768]{2,1,0:T(8,128)} %get-tuple-element.14), channel_id=1, source_target_pairs={{0,1},{1,2},{2,3},{3,4},{4,5},{5,6},{6,7},{8,9},{9,10},{10,11},{11... | collective-permute-start | bytes 1769480 | tf_op jit(solution)/shard_map/ppermute | solution.py:23
  88.4 1.3 collective-permute-start.7
  89.7 0.1 copy.10
  89.8 0.3 collective-permute-done.6
  90.2 7.5 %collective-permute-done.7 = f32[6,32,768]{2,1,0:T(8,128)} collective-permute-done((f32[6,32,768]{2,1,0:T(8,128)}, f32[6,32,768]{2,1,0:T(8,128)}, u32[]{:S(2)}, u32[]{:S(2)}) %collective-permute-start.7) | collective-permute-done | bytes 589856 | tf_op jit(solution)/shard_map/ppermute | solution.py:24
  97.7 1.4 fusion.2
  99.1 0.2 copy.11
  99.2 0.9 fusion.3.dq_ref
  100.1 1.5 convolution_convert_fusion.1
  101.6 1.9 %copy-done.1 = bf16[2048,768]{1,0:T(8,128)(2,1)S(1)} copy-done((bf16[2048,768]{1,0:T(8,128)(2,1)S(1)}, bf16[2048,768]{1,0:T(8,128)(2,1)}, u32[]{:S(2)}) %copy-start.1) | copy-done | bytes 3145752
  103.5 1.1 copy-done.2
  104.5 44.6 %shard_map.51 = bf16[1152,768]{1,0:T(8,128)(2,1)S(1)} custom-call(bf16[2048,768]{1,0:T(8,128)(2,1)S(1)} %copy-done.1, bf16[1152,256]{1,0:T(8,128)(2,1)S(1)} %copy-done.2), custom_call_target="tpu_custom_call" | custom-call | flops 452984832 | bytes 8388608 | tf_op jit(solution)/shard_map/pallas_call | solution.py:246
  149.2 2.2 %copy.12 = bf16[768,1152]{1,0:T(8,128)(2,1)} copy(bf16[768,1152]{0,1:T(8,128)(2,1)S(1)} %bitcast.11) | data formatting | bytes 3538944
  (18 shorter events, 0.1 us)
Async XLA Ops:
  7.2 1.5 copy-start
  7.2 94.4 %all-gather.2.cloned.1.call-start = ((), (), s32[]{:S(2)}) async-start(), calls=%async_computation | async-start | bytes 3538944 | tf_op jit(solution)/shard_map/all_gather | solution.py:278
  10.4 7.1 %collective-permute-start = (bf16[8,6,768]{2,1,0:T(8,128)(2,1)S(1)}, bf16[8,6,768]{2,1,0:T(8,128)(2,1)S(1)}, u32[]{:S(2)}, u32[]{:S(2)}) collective-permute-start(bf16[8,6,768]{2,1,0:T(8,128)(2,1)S(1)} %get-tuple-element.18), channel_id=1, source_target_pairs={{0,8},{8,16},{16,24},{1,9},{9,17},{17,25},{2,10},{10,18},{18,26},{... | collective-permute-start | bytes 221192 | tf_op jit(solution)/shard_map/ppermute | solution.py:23
  15.3 6.5 %collective-permute-start.1 = (bf16[8,6,768]{2,1,0:T(8,128)(2,1)S(1)}, bf16[8,6,768]{2,1,0:T(8,128)(2,1)S(1)}, u32[]{:S(2)}, u32[]{:S(2)}) collective-permute-start(bf16[8,6,768]{2,1,0:T(8,128)(2,1)S(1)} %get-tuple-element.19), channel_id=1, source_target_pairs={{8,0},{16,8},{24,16},{9,1},{17,9},{25,17},{10,2},{18,10},{26,18},{... | collective-permute-start | bytes 221192 | tf_op jit(solution)/shard_map/ppermute | solution.py:24
  22.1 4.2 %collective-permute-start.2 = (bf16[6,44,768]{2,1,0:T(8,128)(2,1)S(1)}, bf16[6,44,768]{2,1,0:T(8,128)(2,1)S(1)}, u32[]{:S(2)}, u32[]{:S(2)}) collective-permute-start(bf16[6,44,768]{2,1,0:T(8,128)(2,1)S(1)} %get-tuple-element.16), channel_id=1, source_target_pairs={{0,1},{1,2},{2,3},{3,4},{4,5},{5,6},{6,7},{8,9},{9,10},{10,11},{11... | collective-permute-start | bytes 1216520 | tf_op jit(solution)/shard_map/ppermute | solution.py:23
  23.4 5.4 %collective-permute-start.3 = (bf16[6,44,768]{2,1,0:T(8,128)(2,1)S(1)}, bf16[6,44,768]{2,1,0:T(8,128)(2,1)S(1)}, u32[]{:S(2)}, u32[]{:S(2)}) collective-permute-start(bf16[6,44,768]{2,1,0:T(8,128)(2,1)S(1)} %get-tuple-element.17), channel_id=1, source_target_pairs={{1,0},{2,1},{3,2},{4,3},{5,4},{6,5},{7,6},{9,8},{10,9},{11,10},{12... | collective-permute-start | bytes 1216520 | tf_op jit(solution)/shard_map/ppermute | solution.py:24
  32.4 1.0 copy-start.3
  33.4 0.9 copy-start.4
  34.3 0.9 copy-start.5
  35.2 0.9 copy-start.6
  55.9 9.7 %collective-permute-start.4 = (f32[20,6,768]{2,1,0:T(8,128)S(1)}, f32[20,6,768]{2,1,0:T(8,128)S(1)}, u32[]{:S(2)}, u32[]{:S(2)}) collective-permute-start(f32[20,6,768]{2,1,0:T(8,128)S(1)} %get-tuple-element.12), channel_id=1, source_target_pairs={{0,8},{8,16},{16,24},{1,9},{9,17},{17,25},{2,10},{10,18},{18,26},{... | collective-permute-start | bytes 1105928 | tf_op jit(solution)/shard_map/ppermute | solution.py:23
  59.3 10.7 %collective-permute-start.5 = (f32[20,6,768]{2,1,0:T(8,128)S(1)}, f32[20,6,768]{2,1,0:T(8,128)S(1)}, u32[]{:S(2)}, u32[]{:S(2)}) collective-permute-start(f32[20,6,768]{2,1,0:T(8,128)S(1)} %get-tuple-element.13), channel_id=1, source_target_pairs={{8,0},{16,8},{24,16},{9,1},{17,9},{25,17},{10,2},{18,10},{26,18},{... | collective-permute-start | bytes 1105928 | tf_op jit(solution)/shard_map/ppermute | solution.py:24
  72.0 1.3 copy-start.7
  74.5 15.7 %collective-permute-start.6 = (f32[6,32,768]{2,1,0:T(8,128)}, f32[6,32,768]{2,1,0:T(8,128)S(1)}, u32[]{:S(2)}, u32[]{:S(2)}) collective-permute-start(f32[6,32,768]{2,1,0:T(8,128)} %get-tuple-element.14), channel_id=1, source_target_pairs={{0,1},{1,2},{2,3},{3,4},{4,5},{5,6},{6,7},{8,9},{9,10},{10,11},{11... | collective-permute-start | bytes 1769480 | tf_op jit(solution)/shard_map/ppermute | solution.py:23
  88.4 9.3 %collective-permute-start.7 = (f32[6,32,768]{2,1,0:T(8,128)}, f32[6,32,768]{2,1,0:T(8,128)}, u32[]{:S(2)}, u32[]{:S(2)}) collective-permute-start(f32[6,32,768]{2,1,0:T(8,128)} %get-tuple-element.15), channel_id=1, source_target_pairs={{1,0},{2,1},{3,2},{4,3},{5,4},{6,5},{7,6},{9,8},{10,9},{11,10},{12... | collective-permute-start | bytes 1769480 | tf_op jit(solution)/shard_map/ppermute | solution.py:24
  101.6 1.9 %copy-start.1 = (bf16[2048,768]{1,0:T(8,128)(2,1)S(1)}, bf16[2048,768]{1,0:T(8,128)(2,1)}, u32[]{:S(2)}) copy-start(bf16[2048,768]{1,0:T(8,128)(2,1)} %all-gather.2.cloned.1.call-done.tok_ref) | copy-start | bytes 9437188
  103.5 1.1 copy-start.2
Sparse Core Ops, SparseCore 0:
  9.9 37.4 all-gather.1

commit v2 on v1

--- a/solution.py
+++ b/solution.py
@@ -2,6 +2,7 @@
 
 import jax
 import jax.numpy as jnp
+import numpy as np
 from jax import lax
 from jax.experimental import pallas as pl
 from jax.experimental.pallas import tpu as pltpu
@@ -13,79 +14,216 @@
 MESH = pl.DeviceIdType.MESH
 
 
-def padded(value, sides, width):
-    for axis, dim in sides:
-        size, length = (lax.axis_size(axis), value.shape[dim])
-        up = [(i, (i + 1) % size) for i in range(size - 1)]
-        down = [(j, i) for i, j in up]
-        last = lax.slice_in_dim(value, length - width, length, axis=dim)
-        leading = lax.slice_in_dim(value, 0, width, axis=dim)
-        before = lax.ppermute(last, axis, up)
-        after = lax.ppermute(leading, axis, down)
-        value = jnp.concatenate([before, value, after], axis=dim)
-    return value
-
-
-def attention_kernel(nb, qr, qc, kr, kc, q_ref, k_ref, v_ref, g_ref, dq_ref, dk_ref, dv_ref):
-    count = q_ref.shape[0] // nb
-    span = kr.shape[2]
-    step = (k_ref.shape[0] - span) // max(nb - 1, 1)
-    dk_ref[...] = jnp.zeros_like(dk_ref)
-    dv_ref[...] = jnp.zeros_like(dv_ref)
-    for b in range(nb):
-        rows = pl.ds(b * count, count)
-        keys = pl.ds(b * step, span)
-        ok = (jnp.abs(qr[rows, :] - kr[b]) <= RADIUS) & (jnp.abs(qc[rows, :] - kc[b]) <= RADIUS)
-        bias = jnp.where(ok, 0.0, -1e30)
-        q8 = q_ref[rows, :] * jnp.bfloat16(HDIM ** -0.5)
-        kb, vb, g = k_ref[keys, :], v_ref[keys, :], g_ref[rows, :]
-        dqs, dks, dvs = [], [], []
-        for h in range(2):
-            cols = slice(h * HDIM, (h + 1) * HDIM)
-            qh, kh, vh, gh = q8[:, cols], kb[:, cols], vb[:, cols], g[:, cols]
-            nt = (((1,), (1,)), ((), ()))
-            tn = (((0,), (0,)), ((), ()))
-            dot = functools.partial(lax.dot_general, preferred_element_type=jnp.float32)
-            s = dot(qh, kh, nt) + bias
-            e = jnp.exp(s - jnp.max(s, axis=1, keepdims=True))
-            p = e * (1.0 / jnp.sum(e, axis=1, keepdims=True))
-            pb = p.astype(jnp.bfloat16)
-            att = jnp.dot(pb, vh, preferred_element_type=jnp.float32)
-            delta = jnp.sum(gh.astype(jnp.float32) * att, axis=1, keepdims=True)
-            dp = dot(gh, vh, nt)
-            ds = (p * (dp - delta)).astype(jnp.bfloat16)
-            dqs.append(jnp.dot(ds, kh, preferred_element_type=jnp.float32) * (HDIM ** -0.5))
-            dks.append(dot(ds, qh, tn))
-            dvs.append(dot(pb, gh, tn))
-        dq_ref[rows, :] = jnp.concatenate(dqs, axis=1)
-        dk_ref[keys, :] += jnp.concatenate(dks, axis=1)
-        dv_ref[keys, :] += jnp.concatenate(dvs, axis=1)
-
-
-def attention(q, kv, g, qr, qc, kr, kc, nb):
-    count, width = q.shape
-    extent = kv.shape[0]
-    lanes = 2 * HDIM
-    groups = width // lanes
-    whole = lambda a: pl.BlockSpec(a.shape, lambda i: (0,) * a.ndim)
-    qs = pl.BlockSpec((count, lanes), lambda i: (0, i))
-    ks = pl.BlockSpec((extent, lanes), lambda i: (0, i))
-    vs = pl.BlockSpec((extent, lanes), lambda i: (0, i + groups))
+DIRS = [(dn, de) for dn in (-1, 0, 1) for de in (-1, 0, 1) if (dn, de) != (0, 0)]
+
+
+def halo_attention_kernel(
+    nn, ne, qr, qc, kr, kc, qkv_ref, first_ref, last_ref, g_ref, out_ref, ext, acc, *rest
+):
+    back = rest[:8]
+    f_send, f_recv, b_send, b_recv = rest[8:]
+    e, n = lax.axis_index("ew"), lax.axis_index("ns")
+    pairs, wide, total = qkv_ref.shape
+    width = total // 3
+    half = RADIUS // 2
+    groups, lanes = width // 128, 128
+    slots = ext.shape[1]
+    side = (slots - wide) // 2
+    nb = kr.shape[0]
+    step = pairs // nb
+    tall = step + 2 * half
+    cols = wide // 2
+
+    def exists(d):
+        dn, de = d
+        return (n + dn >= 0) & (n + dn < nn) & (e + de >= 0) & (e + de < ne)
+
+    def own_pairs(dn):
+        return {-1: pl.ds(0, half), 0: pl.ds(0, pairs), 1: pl.ds(pairs - half, half)}[dn]
+
+    def region(d):
+        rows = {-1: pl.ds(0, half), 0: pl.ds(half, pairs), 1: pl.ds(half + pairs, half)}[d[0]]
+        place = {0: pl.ds(0, wide), 1: pl.ds(wide, side), -1: pl.ds(wide + side, side)}[d[1]]
+        return rows, place
+
+    def opposite(i):
+        return DIRS.index((-DIRS[i][0], -DIRS[i][1]))
+
+    def forward(i):
+        dn, de = DIRS[i]
+        rows = own_pairs(dn)
+        if de == 0:
+            src = qkv_ref.at[rows, :, pl.ds(width, 2 * width)]
+        else:
+            src = (first_ref if de < 0 else last_ref).at[rows]
+        there = opposite(i)
+        a, b = region(DIRS[there])
+        return pltpu.make_async_remote_copy(
+            src_ref=src, dst_ref=ext.at[a, b], send_sem=f_send.at[i], recv_sem=f_recv.at[there],
+            device_id=(e + de, n + dn), device_id_type=MESH,
+        )
+
+    def forward_in(i):
+        a, b = region(DIRS[i])
+        return pltpu.make_async_remote_copy(
+            src_ref=ext.at[a, b], dst_ref=ext.at[a, b], send_sem=f_send.at[i], recv_sem=f_recv.at[i],
+            device_id=(e + DIRS[i][1], n + DIRS[i][0]), device_id_type=MESH,
+        )
+
+    def backward(i, grp):
+        a, b = region(DIRS[i])
+        there = opposite(i)
+        return pltpu.make_async_remote_copy(
+            src_ref=acc.at[grp, a, b], dst_ref=back[there].at[grp],
+            send_sem=b_send.at[i, grp], recv_sem=b_recv.at[there, grp],
+            device_id=(e + DIRS[i][1], n + DIRS[i][0]), device_id_type=MESH,
+        )
+
+    def backward_in(i, grp):
+        return pltpu.make_async_remote_copy(
+            src_ref=back[i].at[grp], dst_ref=back[i].at[grp],
+            send_sem=b_send.at[i, grp], recv_sem=b_recv.at[i, grp],
+            device_id=(e + DIRS[i][1], n + DIRS[i][0]), device_id_type=MESH,
+        )
+
+    barrier = pltpu.get_barrier_semaphore()
+    for d in DIRS:
+
+        @pl.when(exists(d))
+        def _():
+            pl.semaphore_signal(barrier, inc=1, device_id=(e + d[1], n + d[0]), device_id_type=MESH)
+
+    pl.semaphore_wait(barrier, sum(exists(d).astype(jnp.int32) for d in DIRS))
+
+    for i, d in enumerate(DIRS):
+
+        @pl.when(exists(d))
+        def _():
+            forward(i).start()
+
+    ext[pl.ds(half, pairs), pl.ds(0, wide), :] = qkv_ref[:, :, pl.ds(width, 2 * width)]
+    acc[...] = jnp.zeros_like(acc)
+    for i, d in enumerate(DIRS):
+        a, b = region(d)
+
+        @pl.when(jnp.logical_not(exists(d)))
+        def _():
+            ext[a, b, :] = jnp.zeros((a.size, b.size, 2 * width), ext.dtype)
+
+        @pl.when(exists(d))
+        def _():
+            forward_in(i).wait_recv()
+
+    nt = (((1,), (1,)), ((), ()))
+    tn = (((0,), (0,)), ((), ()))
+    dot = functools.partial(lax.dot_general, preferred_element_type=jnp.float32)
+    count = step * wide
+
+    def one_group(grp, carry):
+        at = pl.multiple_of(grp * lanes, lanes)
+        at_v = pl.multiple_of(grp * lanes + width, lanes)
+        for b in range(nb):
+            rows = pl.ds(b * step, step)
+            keys = pl.ds(b * step, tall)
+            flat = pl.ds(b * count, count)
+            ok = (jnp.abs(qr[flat, :] - kr[b]) <= RADIUS) & (jnp.abs(qc[flat, :] - kc[b]) <= RADIUS)
+            bias = jnp.where(ok, 0.0, -1e30)
+            q8 = qkv_ref[rows, :, pl.ds(at, lanes)].reshape(count, lanes) * jnp.bfloat16(HDIM ** -0.5)
+            g = g_ref[rows, :, pl.ds(at, lanes)].reshape(count, lanes)
+            kb = ext[keys, :, pl.ds(at, lanes)].reshape(tall * slots, lanes)
+            vb = ext[keys, :, pl.ds(at_v, lanes)].reshape(tall * slots, lanes)
+            dqs, dks, dvs = [], [], []
+            for h in range(2):
+                part = slice(h * HDIM, (h + 1) * HDIM)
+                qh, kh, vh, gh = q8[:, part], kb[:, part], vb[:, part], g[:, part]
+                s = dot(qh, kh, nt) + bias
+                ex = jnp.exp(s - jnp.max(s, axis=1, keepdims=True))
+                p = ex * (1.0 / jnp.sum(ex, axis=1, keepdims=True))
+                pb = p.astype(jnp.bfloat16)
+                att = jnp.dot(pb, vh, preferred_element_type=jnp.float32)
+                delta = jnp.sum(gh.astype(jnp.float32) * att, axis=1, keepdims=True)
+                dp = dot(gh, vh, nt)
+                ds = (p * (dp - delta)).astype(jnp.bfloat16)
+                dqs.append(jnp.dot(ds, kh, preferred_element_type=jnp.float32) * (HDIM ** -0.5))
+                dks.append(dot(ds, qh, tn))
+                dvs.append(dot(pb, gh, tn))
+            dq = jnp.concatenate(dqs, axis=1).astype(out_ref.dtype)
+            out_ref[rows, :, pl.ds(at, lanes)] = dq.reshape(step, wide, lanes)
+            both = jnp.concatenate(dks + dvs, axis=1).reshape(tall, slots, 2 * lanes)
+            acc[grp, keys] += both
+        for i, d in enumerate(DIRS):
+
+            @pl.when(exists(d))
+            def _():
+                backward(i, grp).start()
+
+        return carry
+
+    lax.fori_loop(0, groups, one_group, 0)
+
+    def collect(grp, carry):
+        for i, d in enumerate(DIRS):
+            mine = own_pairs(d[0])
+            here = pl.ds(half + mine.start, mine.size)
+
+            @pl.when(exists(d))
+            def _():
+                backward_in(i, grp).wait_recv()
+                if d[1] == 0:
+                    acc[grp, here, pl.ds(0, wide)] += back[i][grp]
+                else:
+                    for r in range(2):
+                        to = r * cols + (0 if d[1] < 0 else cols - side // 2)
+                        acc[grp, here, pl.ds(to, side // 2)] += back[i][grp, :, pl.ds(r * side // 2, side // 2)]
+
+        for j in range(2):
+            to = pl.multiple_of(grp * lanes + (j + 1) * width, lanes)
+            own = acc[grp, pl.ds(half, pairs), pl.ds(0, wide), pl.ds(j * lanes, lanes)]
+            out_ref[:, :, pl.ds(to, lanes)] = own.astype(out_ref.dtype)
+        return carry
+
+    lax.fori_loop(0, groups, collect, 0)
+
+    for i, d in enumerate(DIRS):
+
+        @pl.when(exists(d))
+        def _():
+            forward(i).wait_send()
+            for grp in range(groups):
+                backward(i, grp).wait_send()
+
+
+def halo_attention(qkv, first, last, g, qr, qc, kr, kc, slots, nn, ne):
+    pairs, wide, total = qkv.shape
+    half, width = RADIUS // 2, total // 3
+    groups, side = width // 128, (slots - wide) // 2
+    tall = pairs + 2 * half
+    dma = pltpu.SemaphoreType.DMA
+    vm = pl.BlockSpec(memory_space=pltpu.VMEM)
+    back = [
+        pltpu.VMEM((groups, half if dn else pairs, side if de else wide, 256), jnp.float32)
+        for dn, de in DIRS
+    ]
     return pl.pallas_call(
-        functools.partial(attention_kernel, nb),
-        grid=(groups,),
-        in_specs=[whole(qr), whole(qc), whole(kr), whole(kc), qs, ks, vs, qs],
-        out_specs=[qs, ks, ks],
-        out_shape=[
-            jax.ShapeDtypeStruct((count, width), jnp.float32),
-            jax.ShapeDtypeStruct((extent, width), jnp.float32),
-            jax.ShapeDtypeStruct((extent, width), jnp.float32),
-        ],
-        compiler_params=pltpu.CompilerParams(vmem_limit_bytes=40 << 20),
+        functools.partial(halo_attention_kernel, nn, ne),
+        out_shape=jax.ShapeDtypeStruct(qkv.shape, jnp.bfloat16),
+        in_specs=[vm] * 8,
+        out_specs=vm,
+        scratch_shapes=[
+            pltpu.VMEM((tall, slots, 2 * width), jnp.bfloat16),
+            pltpu.VMEM((groups, tall, slots, 256), jnp.float32),
+        ]
+        + back
+        + [dma((8,)), dma((8,)), dma((8, groups)), dma((8, groups))],
+        compiler_params=pltpu.CompilerParams(
+            collective_id=2, has_side_effects=True, vmem_limit_bytes=44 << 20
+        ),
         cost_estimate=pl.CostEstimate(
-            flops=14 * count * extent * width, bytes_accessed=8 << 20, transcendentals=count * extent * HEADS
+            flops=14 * pairs * wide * tall * slots * width,
+            bytes_accessed=4 << 20,
+            transcendentals=pairs * wide * tall * slots * HEADS,
         ),
-    )(qr, qc, kr, kc, q, kv, kv, g)
+    )(qr, qc, kr, kc, qkv, first, last, g)
 
 
 CH = 128
@@ -277,44 +415,36 @@
     if paired:
         tok_all = lax.all_gather(flat_tokens, "ns", axis=0, tiled=True)
     projected = jnp.dot(flat_tokens, w_qkv, preferred_element_type=jnp.float32).astype(jnp.bfloat16)
-    wide_kv = padded(
-        projected[:, width:].reshape(tile_rows, tile_cols, 2 * width),
-        (("ew", 1), ("ns", 0)),
-        RADIUS,
-    )
-    ext_rows, ext_cols = (wide_kv.shape[0], wide_kv.shape[1])
-    key_values = wide_kv.reshape(ext_rows * ext_cols, 2 * width)
+    half, pairs, wide, edge = RADIUS // 2, tile_rows // 2, 2 * tile_cols, 8
+    slots = wide + 4 * edge
+    qkv = projected.reshape(pairs, wide, 3 * width)
+    by_row = projected[:, width:].reshape(tile_rows, tile_cols, 2 * width)
+    first = by_row[:, :edge].reshape(pairs, 2 * edge, 2 * width)
+    last = by_row[:, tile_cols - edge :].reshape(pairs, 2 * edge, 2 * width)
     nb = 2
     row0 = lax.axis_index("ns") * tile_rows
     col0 = lax.axis_index("ew") * tile_cols
     qi = jnp.arange(count, dtype=jnp.int32)
     qr = (row0 + qi // tile_cols)[:, None]
     qc = (col0 + qi % tile_cols)[:, None]
-    ki = jnp.arange(ext_rows * ext_cols, dtype=jnp.int32)
-    kr = row0 - RADIUS + ki // ext_cols
-    kc = col0 - RADIUS + ki % ext_cols
+    slot = np.arange(slots)
+    in_side = np.maximum(slot - wide, 0)
+    slot_row = np.where(slot < wide, slot // tile_cols, (in_side % (2 * edge)) // edge)
+    slot_col = np.where(
+        slot < wide,
+        slot % tile_cols,
+        np.where(in_side < 2 * edge, tile_cols + in_side % edge, in_side % edge - edge),
+    )
+    ext_row = (2 * np.arange(pairs + 2 * half)[:, None] - RADIUS + slot_row[None]).astype(np.int32)
+    ext_col = np.broadcast_to(slot_col[None], ext_row.shape).astype(np.int32)
+    kr, kc = row0 + ext_row, col0 + ext_col
     inside = (kr >= 0) & (kr < nn * tile_rows) & (kc >= 0) & (kc < ne * tile_cols)
     kr = jnp.where(inside, kr, -1000)
-    per = tile_rows // nb
-    span = (per + 2 * RADIUS) * ext_cols
-    pick = lambda a: jnp.stack([a[b * per * ext_cols :][:span][None] for b in range(nb)])
-    query_grad, key_grad, value_grad = attention(
-        projected[:, :width], key_values, grad_out.reshape(count, width), qr, qc, pick(kr), pick(kc), nb
-    )
-    ext_grads = jnp.concatenate([key_grad, value_grad], axis=1).reshape(ext_rows, ext_cols, 2 * width)
-    side_strips = jnp.concatenate([ext_grads[:, :RADIUS], ext_grads[:, tile_cols + RADIUS :]], axis=1)
-    from_sides = padded(side_strips, (("ew", 1),), RADIUS)
-    middle = ext_grads[:, RADIUS : tile_cols + RADIUS]
-    middle = middle + jnp.pad(from_sides[:, :RADIUS], ((0, 0), (0, tile_cols - RADIUS), (0, 0)))
-    middle = middle + jnp.pad(from_sides[:, 3 * RADIUS :], ((0, 0), (tile_cols - RADIUS, 0), (0, 0)))
-    edge_strips = jnp.concatenate([middle[:RADIUS], middle[tile_rows + RADIUS :]], axis=0)
-    from_edges = padded(edge_strips, (("ns", 0),), RADIUS)
-    owned = middle[RADIUS : tile_rows + RADIUS]
-    owned = owned + jnp.pad(from_edges[:RADIUS], ((0, tile_rows - RADIUS), (0, 0), (0, 0)))
-    owned = owned + jnp.pad(from_edges[3 * RADIUS :], ((tile_rows - RADIUS, 0), (0, 0), (0, 0)))
-    dqkv = jnp.concatenate([query_grad, owned.reshape(count, 2 * width)], axis=1).astype(
-        jnp.bfloat16
-    )
+    per = pairs // nb
+    pick = lambda a: jnp.stack([a[b * per : b * per + per + 2 * half].reshape(1, -1) for b in range(nb)])
+    dqkv = halo_attention(
+        qkv, first, last, grad_out.reshape(pairs, wide, width), qr, qc, pick(kr), pick(kc), slots, nn, ne
+    ).reshape(count, 3 * width)
     grad_tokens = (
         jnp.dot(dqkv, w_qkv.T, preferred_element_type=jnp.float32)
         .astype(jnp.bfloat16)

time: 161 us -> 111 us (0.69)
  starting transfers between devices: 28.8 us -> 0.04 us
  Pallas kernels: 57.4 us -> 76.6 us
  waiting for transfers between devices: 25.6 us -> 7.72 us
  local copies, waits for them, and re-layouts: 20.7 us -> 6.61 us
  other arithmetic: 8.37 us -> 0.76 us
    ppermute x8 -> x0, starting transfers between devices: 28.8 us -> none  [the longest x4 23.6 us: padded(): before = lax.ppermute(last, axis, up)]
    ppermute x8 -> x0, waiting for transfers between devices: 24.9 us -> none  [the longest x4 18.7 us: padded(): after = lax.ppermute(leading, axis, down)]
    pallas_call x1, Pallas kernels: 12.8 us -> 35.2 us  [halo_attention(): pl.pallas_call(functools.partial(halo_attention_kernel, nn, ne), out_shap...]
    all_gather x1, waiting for transfers between devices: 0.01 us -> 7.04 us  [local(): tok_all = lax.all_gather(flat_tokens, 'ns', axis=0, tiled=True)]
    unnamed x17 -> x9, local copies, waits for them, and re-layouts: 11 us -> 5.18 us
    reshape x3 -> x1, local copies, waits for them, and re-layouts: 6.14 us -> 1.06 us  [local(): dqkv = halo_attention(qkv, first, last, grad_out.reshape(pairs, wide, wid...]
    slice x8 -> x3, local copies, waits for them, and re-layouts: 3.48 us -> 0.05 us  [the longest x1 0.03 us: local(): by_row = projected[:, width:].reshape(tile_rows, tile_cols, 2 * width)]
    concatenate x3 -> x0, other arithmetic: 3.3 us -> none  [the longest x1 1.79 us: local(): jnp.concatenate([key_grad, value_grad], axis=1)]
  transfers between devices with their start and end apart: 9 -> 1, of which waited for: 7 -> 1; matrix products, arithmetic and copies ran while one was open for 13% -> 5% of each run, Pallas kernels for 8% -> 32%
where the time goes in v2:
time: 111 us; the launch traced here: 109 us
  Pallas kernels  76.6 us (69%)
  between operations  14.1 us (13%)
  waiting for transfers between devices  7.72 us (7%)
  local copies, waits for them, and re-layouts  6.61 us (6%)
  matrix products  3.18 us (3%)
    pallas_call x1, Pallas kernels, weight_sum(): pl.pallas_call(functools.partial(weight_kernel, nn, ne), out_shape=jax.Sh...  41.4 us
    pallas_call x1, Pallas kernels, halo_attention(): pl.pallas_call(functools.partial(halo_attention_kernel, nn, ne), out_shap...  35.2 us
    all_gather x1, waiting for transfers between devices, local(): tok_all = lax.all_gather(flat_tokens, 'ns', axis=0, tiled=True)  7.04 us
    unnamed x9, local copies, waits for them, and re-layouts  5.18 us
  transfers between devices with their start and end apart: 1, of which 1 were waited for; matrix products, arithmetic and copies ran while one was open for 5% of the time, Pallas kernels for 32%

profile of v2, /device:TPU:0, one launch (start us, length us, event | category | flops | bytes accessed | tf_op | source)
XLA Modules:
  0.0 109.0 jit_solution(4294519566325742582)
XLA Ops:
  7.2 0.0 copy-start
  7.2 0.0 all-gather.2.cloned.1.call-start
  7.2 0.7 all-gather.2.cloned.1.call-update
  7.9 0.7 broadcast_add_fusion
  8.7 0.1 stack_reshape.14
  8.7 0.1 stack_reshape.15
  8.8 0.1 stack_reshape.13
  8.9 0.1 stack_reshape.12
  9.0 0.0 copy-done
  9.0 0.0 copy-start.3
  9.0 1.7 %convolution_convert_fusion = bf16[256,1152]{1,0:T(8,128)(2,1)S(1)} fusion(bf16[256,768]{1,0:T(8,128)(2,1)} %bitcast.24, bf16[768,1152]{1,0:T(8,128)(2,1)S(1)} %copy-done), kind=kOutput, calls=%fused_computation | convolution fusion | flops 453279744 | bytes 2752512 | tf_op jit(solution)/shard_map/dot_general | solution.py:417
  10.8 0.0 copy-done.3
  10.8 35.2 %shard_map.68 = bf16[4,64,1152]{2,1,0:T(8,128)(2,1)S(1)} custom-call(s32[256,1]{1,0:T(8,128)S(1)} %get-tuple-element.16.qr, s32[256,1]{1,0:T(8,128)S(1)} %get-tuple-element.17.qc, s32[2,1,768]{2,1,0:T(1,128)S(1)} %pad_add_fusion.kr, s32[2,1,768]{2,1,0:T(1,128)S(1)} %pad_add_fusion.1.kc, bf16[4,64,1152]{2,1,0:T(8,128)(2,1)S(1)} %bitcast.18, ...), custom_call_target="tpu_custom_call" | custom-call | flops 1321205760 | bytes 4194304 | tf_op jit(solution)/shard_map/pallas_call | solution.py:207
  46.0 1.1 copy.9
  47.1 1.5 %convolution_convert_fusion.1 = bf16[256,768]{1,0:T(8,128)(2,1)} fusion(bf16[256,1152]{1,0:T(8,128)(2,1)S(1)} %bitcast.17, bf16[768,1152]{1,0:T(8,128)(2,1)S(1)} %copy-done), kind=kOutput, calls=%fused_computation.1 | convolution fusion | flops 453181440 | bytes 2752512 | tf_op jit(solution)/shard_map/dot_general | solution.py:449
  48.6 7.0 %all-gather.2.cloned.1.call-done.tok_ref = bf16[2048,768]{1,0:T(8,128)(2,1)} async-done(((bf16[256,768]{1,0:T(8,128)(2,1)}), bf16[2048,768]{1,0:T(8,128)(2,1)}) %all-gather.2.cloned.1.call-update) | async-done | bytes 3145744 | tf_op jit(solution)/shard_map/all_gather | solution.py:416
  55.6 0.0 copy-start.1
  55.6 1.9 %copy-done.1 = bf16[2048,768]{1,0:T(8,128)(2,1)S(1)} copy-done((bf16[2048,768]{1,0:T(8,128)(2,1)S(1)}, bf16[2048,768]{1,0:T(8,128)(2,1)}, u32[]{:S(2)}) %copy-start.1) | copy-done | bytes 3145752
  57.5 0.0 copy-start.2
  57.5 1.1 copy-done.2
  58.5 41.4 %shard_map.69 = bf16[1152,768]{1,0:T(8,128)(2,1)S(1)} custom-call(bf16[2048,768]{1,0:T(8,128)(2,1)S(1)} %copy-done.1, bf16[1152,256]{1,0:T(8,128)(2,1)S(1)} %bitcast.15), custom_call_target="tpu_custom_call" | custom-call | flops 452984832 | bytes 8388608 | tf_op jit(solution)/shard_map/pallas_call | solution.py:384
  100.0 2.2 %copy.10 = bf16[768,1152]{1,0:T(8,128)(2,1)} copy(bf16[768,1152]{0,1:T(8,128)(2,1)S(1)} %bitcast.14) | data formatting | bytes 3538944
  (6 shorter events, 0.1 us)
Async XLA Ops:
  7.2 1.8 %copy-start = (bf16[768,1152]{1,0:T(8,128)(2,1)S(1)}, bf16[768,1152]{1,0:T(8,128)(2,1)}, u32[]{:S(2)}) copy-start(bf16[768,1152]{1,0:T(8,128)(2,1)} %param.6) | copy-start | bytes 5308420
  7.2 48.4 %all-gather.2.cloned.1.call-start = ((), (), s32[]{:S(2)}) async-start(), calls=%async_computation | async-start | bytes 3538944 | tf_op jit(solution)/shard_map/all_gather | solution.py:416
  9.0 1.9 %copy-start.3 = (bf16[8,32,384]{2,1,0:T(8,128)(2,1)S(1)}, bf16[8,32,384]{2,1,0:T(8,128)(2,1)}, u32[]{:S(2)}) copy-start(bf16[8,32,384]{2,1,0:T(8,128)(2,1)} %param.7) | copy-start | bytes 589828
  55.6 1.9 %copy-start.1 = (bf16[2048,768]{1,0:T(8,128)(2,1)S(1)}, bf16[2048,768]{1,0:T(8,128)(2,1)}, u32[]{:S(2)}) copy-start(bf16[2048,768]{1,0:T(8,128)(2,1)} %all-gather.2.cloned.1.call-done.tok_ref) | copy-start | bytes 9437188
  57.5 1.1 copy-start.2
Sparse Core Ops, SparseCore 0:
  9.9 45.6 all-gather.1

commit v3 on v2

--- a/solution.py
+++ b/solution.py
@@ -18,7 +18,7 @@
 
 
 def halo_attention_kernel(
-    nn, ne, qr, qc, kr, kc, qkv_ref, first_ref, last_ref, g_ref, out_ref, ext, acc, *rest
+    nn, ne, more, qr, qc, kr, kc, qkv_ref, first_ref, last_ref, g_ref, out_ref, ext, acc, *rest
 ):
     back = rest[:8]
     f_send, f_recv, b_send, b_recv = rest[8:]
@@ -86,14 +86,22 @@
             device_id=(e + DIRS[i][1], n + DIRS[i][0]), device_id_type=MESH,
         )
 
+    near = DIRS
     barrier = pltpu.get_barrier_semaphore()
-    for d in DIRS:
+    if more is not None:
+        near = [d for d in DIRS if d[0] and d[1]]
+        for k in range(1, nn):
+            pl.semaphore_signal(barrier, inc=1, device_id=(e, lax.rem(n + k, nn)), device_id_type=MESH)
+        for k in range(1, ne):
+            pl.semaphore_signal(barrier, inc=1, device_id=(lax.rem(e + k, ne), n), device_id_type=MESH)
+    for d in near:
 
         @pl.when(exists(d))
         def _():
             pl.semaphore_signal(barrier, inc=1, device_id=(e + d[1], n + d[0]), device_id_type=MESH)
 
-    pl.semaphore_wait(barrier, sum(exists(d).astype(jnp.int32) for d in DIRS))
+    others = nn - 1 + ne - 1 if more is not None else 0
+    pl.semaphore_wait(barrier, others + sum(exists(d).astype(jnp.int32) for d in near))
 
     for i, d in enumerate(DIRS):
 
@@ -114,6 +122,8 @@
         def _():
             forward_in(i).wait_recv()
 
+    if more is not None:
+        more.start()
     nt = (((1,), (1,)), ((), ()))
     tn = (((0,), (0,)), ((), ()))
     dot = functools.partial(lax.dot_general, preferred_element_type=jnp.float32)
@@ -147,8 +157,10 @@
                 dqs.append(jnp.dot(ds, kh, preferred_element_type=jnp.float32) * (HDIM ** -0.5))
                 dks.append(dot(ds, qh, tn))
                 dvs.append(dot(pb, gh, tn))
-            dq = jnp.concatenate(dqs, axis=1).astype(out_ref.dtype)
-            out_ref[rows, :, pl.ds(at, lanes)] = dq.reshape(step, wide, lanes)
+            dq = jnp.concatenate(dqs, axis=1)
+            if more is not None:
+                more.turned[pl.ds(at, lanes), pl.ds(b * count, count)] = dq.T.astype(out_ref.dtype)
+            out_ref[rows, :, pl.ds(at, lanes)] = dq.astype(out_ref.dtype).reshape(step, wide, lanes)
             both = jnp.concatenate(dks + dvs, axis=1).reshape(tall, slots, 2 * lanes)
             acc[grp, keys] += both
         for i, d in enumerate(DIRS):
@@ -160,6 +172,8 @@
         return carry
 
     lax.fori_loop(0, groups, one_group, 0)
+    if more is not None:
+        more.forward()
 
     def collect(grp, carry):
         for i, d in enumerate(DIRS):
@@ -179,10 +193,14 @@
         for j in range(2):
             to = pl.multiple_of(grp * lanes + (j + 1) * width, lanes)
             own = acc[grp, pl.ds(half, pairs), pl.ds(0, wide), pl.ds(j * lanes, lanes)]
+            if more is not None:
+                more.turned[pl.ds(to, lanes), :] = own.reshape(pairs * wide, lanes).T.astype(out_ref.dtype)
             out_ref[:, :, pl.ds(to, lanes)] = own.astype(out_ref.dtype)
         return carry
 
     lax.fori_loop(0, groups, collect, 0)
+    if more is not None:
+        more.finish()
 
     for i, d in enumerate(DIRS):
 
@@ -205,7 +223,7 @@
         for dn, de in DIRS
     ]
     return pl.pallas_call(
-        functools.partial(halo_attention_kernel, nn, ne),
+        functools.partial(halo_attention_kernel, nn, ne, None),
         out_shape=jax.ShapeDtypeStruct(qkv.shape, jnp.bfloat16),
         in_specs=[vm] * 8,
         out_specs=vm,
@@ -230,7 +248,7 @@
 
 
 def weight_kernel(
-    nn, ne, tok_ref, dq_ref, out_ref, recv, part, slots,
+    nn, ne, mid, tok_ref, dq_ref, out_ref, recv, part, slots,
     a_send, a_recv, r_send, r_recv, z_send, z_recv, p_send, p_recv, f_send, f_recv,
 ):
     e, n = lax.axis_index("ew"), lax.axis_index("ns")
@@ -248,13 +266,6 @@
     def at(d, m):
         return (d, m)
 
-    barrier = pltpu.get_barrier_semaphore()
-    for k in range(1, nn):
-        pl.semaphore_signal(barrier, inc=1, device_id=at(e, lax.rem(n + k, nn)), device_id_type=MESH)
-    for k in range(1, ne):
-        pl.semaphore_signal(barrier, inc=1, device_id=at(lax.rem(e + k, ne), n), device_id_type=MESH)
-    pl.semaphore_wait(barrier, nn - 1 + ne - 1)
-
     def exchange(k):
         to = lax.rem(n + k, nn)
         return pltpu.make_async_remote_copy(
@@ -274,6 +285,7 @@
     for k in range(1, nn):
         exchange(k).start()
     recv[n] = dq_ref[rows_of(n), :]
+    mid()
     for k in range(1, nn):
         arrived(k).wait_recv()
 
@@ -375,18 +387,103 @@
             plane_copy(c, n, sibling, f_send, k, f_recv).wait_send()
 
 
-def weight_sum(tok_all, dqkv_t, nn, ne):
-    wide, count = dqkv_t.shape
-    features = tok_all.shape[1]
-    share, chunks = wide // nn, features // CH
+class More:
+    def __init__(self, nn, ne, tok, w, gt, gw, everything, dqkv, turned, sems, rest):
+        self.nn, self.ne, self.tok, self.w, self.gt, self.gw = nn, ne, tok, w, gt, gw
+        self.everything, self.dqkv, self.turned, self.rest = everything, dqkv, turned, rest
+        self.t_send, self.t_recv, self.u_send, self.u_recv = sems
+        self.e, self.n = lax.axis_index("ew"), lax.axis_index("ns")
+        self.sibling = self.n + 1 - 2 * lax.rem(self.n, 2)
+        self.count = tok.shape[0]
+
+    def block(self, m):
+        return pl.ds(pl.multiple_of(m * self.count, self.count), self.count)
+
+    def peer(self, k, base=None):
+        return self.sibling if k == 0 else lax.rem((self.n if base is None else base) + 2 * k, self.nn)
+
+    def send(self, k):
+        return pltpu.make_async_remote_copy(
+            src_ref=self.tok, dst_ref=self.everything.at[self.block(self.n)],
+            send_sem=self.t_send.at[k], recv_sem=self.t_recv.at[self.n],
+            device_id=(self.e, self.peer(k)), device_id_type=MESH,
+        )
+
+    def pass_on(self, k, m, recv):
+        return pltpu.make_async_remote_copy(
+            src_ref=self.everything.at[self.block(m)], dst_ref=self.everything.at[self.block(m)],
+            send_sem=self.u_send.at[k], recv_sem=recv.at[m],
+            device_id=(self.e, self.sibling), device_id_type=MESH,
+        )
+
+    def start(self):
+        for k in range(self.nn // 2):
+            self.send(k).start()
+        self.everything[self.block(self.n), :] = self.tok[...]
+
+    def forward(self):
+        for k in range(1, self.nn // 2):
+            self.pass_on(k, self.peer(k), self.t_recv).wait_recv()
+            self.pass_on(k, self.peer(k), self.u_recv).start()
+
+    def mid(self):
+        dq = self.dqkv[...].reshape(self.count, self.dqkv.shape[2])
+        for c in range(0, self.w.shape[0], 256):
+            self.gt[:, c : c + 256] = lax.dot_general(
+                dq, self.w[c : c + 256, :], (((1,), (1,)), ((), ())), preferred_element_type=jnp.float32
+            ).astype(jnp.bfloat16)
+        self.pass_on(0, self.sibling, self.t_recv).wait_recv()
+        for k in range(1, self.nn // 2):
+            m = lax.rem(self.sibling + 2 * k, self.nn)
+            self.pass_on(k, m, self.u_recv).wait_recv()
+
+    def finish(self):
+        weight_kernel(self.nn, self.ne, self.mid, self.everything, self.turned, self.gw, *self.rest)
+        for k in range(self.nn // 2):
+            self.send(k).wait_send()
+        for k in range(1, self.nn // 2):
+            self.pass_on(k, self.peer(k), self.u_recv).wait_send()
+
+
+def fused_kernel(nn, ne, *refs):
+    qr, qc, kr, kc, qkv, first, last, g, tok, w, gt, gw, everything, dqkv, turned = refs[:15]
+    sems, scratch, rest = refs[15:19], refs[19:33], refs[33:]
+    more = More(nn, ne, tok, w, gt, gw, everything, dqkv, turned, sems, rest)
+    halo_attention_kernel(nn, ne, more, qr, qc, kr, kc, qkv, first, last, g, dqkv, *scratch)
+
+
+def fused(qkv, first, last, g, qr, qc, kr, kc, slots, nn, ne, tok, w):
+    pairs, wide, total = qkv.shape
+    count, features = tok.shape
+    half, width = RADIUS // 2, total // 3
+    groups, side = width // 128, (slots - wide) // 2
+    tall = pairs + 2 * half
+    share, chunks = total // nn, features // CH
     dma = pltpu.SemaphoreType.DMA
     vm = pl.BlockSpec(memory_space=pltpu.VMEM)
+    back = [
+        pltpu.VMEM((groups, half if dn else pairs, side if de else wide, 256), jnp.float32)
+        for dn, de in DIRS
+    ]
     return pl.pallas_call(
-        functools.partial(weight_kernel, nn, ne),
-        out_shape=jax.ShapeDtypeStruct((wide, features), jnp.bfloat16),
-        in_specs=[vm, vm],
-        out_specs=vm,
+        functools.partial(fused_kernel, nn, ne),
+        out_shape=[
+            jax.ShapeDtypeStruct((count, features), jnp.bfloat16),
+            jax.ShapeDtypeStruct((total, features), jnp.bfloat16),
+        ],
+        in_specs=[vm] * 10,
+        out_specs=[vm, vm],
         scratch_shapes=[
+            pltpu.VMEM((nn * count, features), jnp.bfloat16),
+            pltpu.VMEM((pairs, wide, total), jnp.bfloat16),
+            pltpu.VMEM((total, count), jnp.bfloat16),
+            dma((nn // 2,)), dma((nn,)), dma((nn // 2,)), dma((nn,)),
+            pltpu.VMEM((tall, slots, 2 * width), jnp.bfloat16),
+            pltpu.VMEM((groups, tall, slots, 256), jnp.float32),
+        ]
+        + back
+        + [
+            dma((8,)), dma((8,)), dma((8, groups)), dma((8, groups)),
             pltpu.VMEM((nn, share, count), jnp.bfloat16),
             pltpu.VMEM((chunks, share, CH), jnp.float32),
             pltpu.VMEM((2, ne, share, CH), jnp.float32),
@@ -397,12 +494,14 @@
             dma((chunks, nn // 2)), dma((chunks, nn)),
         ],
         compiler_params=pltpu.CompilerParams(
-            collective_id=1, has_side_effects=True, vmem_limit_bytes=40 << 20
+            collective_id=1, has_side_effects=True, vmem_limit_bytes=44 << 20
         ),
         cost_estimate=pl.CostEstimate(
-            flops=2 * share * nn * count * features, bytes_accessed=8 << 20, transcendentals=0
+            flops=14 * pairs * wide * tall * slots * width + 4 * count * features * total,
+            bytes_accessed=8 << 20,
+            transcendentals=pairs * wide * tall * slots * HEADS,
         ),
-    )(tok_all, dqkv_t)
+    )(qr, qc, kr, kc, qkv, first, last, g, tok, w)
 
 
 def local(tokens, w_qkv, grad_out):
@@ -412,8 +511,6 @@
     count = tile_rows * tile_cols
     flat_tokens = tokens.reshape(count, features)
     paired = nn == 8 and ne == 4
-    if paired:
-        tok_all = lax.all_gather(flat_tokens, "ns", axis=0, tiled=True)
     projected = jnp.dot(flat_tokens, w_qkv, preferred_element_type=jnp.float32).astype(jnp.bfloat16)
     half, pairs, wide, edge = RADIUS // 2, tile_rows // 2, 2 * tile_cols, 8
     slots = wide + 4 * edge
@@ -442,21 +539,22 @@
     kr = jnp.where(inside, kr, -1000)
     per = pairs // nb
     pick = lambda a: jnp.stack([a[b * per : b * per + per + 2 * half].reshape(1, -1) for b in range(nb)])
-    dqkv = halo_attention(
+    halo_args = (
         qkv, first, last, grad_out.reshape(pairs, wide, width), qr, qc, pick(kr), pick(kc), slots, nn, ne
-    ).reshape(count, 3 * width)
+    )
+    if paired:
+        grad_tokens, grad_w_t = fused(*halo_args, flat_tokens, w_qkv)
+        return (grad_tokens.reshape(tokens.shape), grad_w_t.T)
+    dqkv = halo_attention(*halo_args).reshape(count, 3 * width)
     grad_tokens = (
         jnp.dot(dqkv, w_qkv.T, preferred_element_type=jnp.float32)
         .astype(jnp.bfloat16)
         .reshape(tile_rows, tile_cols, features)
     )
-    if paired:
-        grad_w = weight_sum(tok_all, dqkv.T, nn, ne).T
-    else:
-        weight_part = lax.dot_general(
-            flat_tokens, dqkv, (((0,), (0,)), ((), ())), preferred_element_type=jnp.float32
-        )
-        grad_w = lax.psum(weight_part, ("ew", "ns")).astype(jnp.bfloat16)
+    weight_part = lax.dot_general(
+        flat_tokens, dqkv, (((0,), (0,)), ((), ())), preferred_element_type=jnp.float32
+    )
+    grad_w = lax.psum(weight_part, ("ew", "ns")).astype(jnp.bfloat16)
     return (grad_tokens, grad_w)
 
 

time: 111 us -> 94.8 us (0.85)
  between operations: 14.1 us -> 0.72 us
  Pallas kernels: 76.6 us -> 85.6 us
  waiting for transfers between devices: 7.72 us -> 0 us
  local copies, waits for them, and re-layouts: 6.61 us -> 3.34 us
    pallas_call x2 -> x1, Pallas kernels: 76.6 us -> 85.6 us  [fused(): pl.pallas_call(functools.partial(fused_kernel, nn, ne), out_shape=[jax.Sh...]
    all_gather x1 -> x0, waiting for transfers between devices: 7.04 us -> none  [local(): tok_all = lax.all_gather(flat_tokens, 'ns', axis=0, tiled=True)]
    unnamed x9 -> x8, local copies, waits for them, and re-layouts: 5.18 us -> 2.98 us
    dot_general x1 -> x0, matrix products: 1.46 us -> none  [local(): jnp.dot(dqkv, w_qkv.T, preferred_element_type=jnp.float32)]
  transfers between devices with their start and end apart: 1 -> 0, of which waited for: 1 -> 0; matrix products, arithmetic and copies ran while one was open for 5% -> 0% of each run, Pallas kernels for 32% -> 0%
where the time goes in v3:
time: 94.8 us; the launch traced here: 92.9 us
  Pallas kernels  85.6 us (90%)
  local copies, waits for them, and re-layouts  3.34 us (4%)
  matrix products  2.43 us (3%)
    pallas_call x1, Pallas kernels, fused(): pl.pallas_call(functools.partial(fused_kernel, nn, ne), out_shape=[jax.Sh...  85.6 us
    unnamed x8, local copies, waits for them, and re-layouts  2.98 us
    dot_general x1, matrix products, local(): jnp.dot(flat_tokens, w_qkv, preferred_element_type=jnp.float32)  2.43 us

profile of v3, /device:TPU:0, one launch (start us, length us, event | category | flops | bytes accessed | tf_op | source)
XLA Modules:
  0.0 92.9 jit_solution(9830347584364097163)
XLA Ops:
  0.6 0.7 broadcast_add_fusion
  1.4 0.1 stack_reshape.14
  1.4 0.1 stack_reshape.15
  1.5 0.1 stack_reshape.13
  1.6 0.1 stack_reshape.12
  1.7 0.0 copy-start
  1.8 0.0 copy-start.1
  1.8 0.0 copy-start.2
  1.8 2.4 %convolution_convert_fusion = bf16[256,1152]{1,0:T(8,128)(2,1)S(1)} fusion(bf16[256,768]{1,0:T(8,128)(2,1)} %bitcast.15, bf16[768,1152]{1,0:T(8,128)(2,1)} %refs_9_.1), kind=kOutput, calls=%fused_computation | convolution fusion | flops 453279744 | bytes 2752512 | tf_op jit(solution)/shard_map/dot_general | solution.py:514
  4.3 0.0 copy-done
  4.3 0.0 copy-done.1
  4.3 0.0 copy-done.2
  4.3 85.6 %shard_map.68 = (bf16[256,768]{1,0:T(8,128)(2,1)S(1)}, bf16[1152,768]{1,0:T(8,128)(2,1)S(1)}) custom-call(s32[256,1]{1,0:T(8,128)S(1)} %get-tuple-element.18.refs_0_, s32[256,1]{1,0:T(8,128)S(1)} %get-tuple-element.19.refs_1_, s32[2,1,768]{2,1,0:T(1,128)S(1)} %pad_add_fusion.refs_2_, s32[2,1,768]{2,1,0:T(1,128)S(1)} %pad_add_fusion.1.refs_3_, ...), custom_call_target="tpu_custom_call" | custom-call | flops 2227175424 | bytes 8388608 | tf_op jit(solution)/shard_map/pallas_call | solution.py:468
  89.9 2.2 %copy.7 = bf16[768,1152]{1,0:T(8,128)(2,1)} copy(bf16[768,1152]{0,1:T(8,128)(2,1)S(1)} %bitcast.10) | data formatting | bytes 3538944
  92.1 0.7 copy.9
  (6 shorter events, 0.1 us)
Async XLA Ops:
  1.7 2.5 %copy-start = (bf16[768,1152]{1,0:T(8,128)(2,1)S(1)}, bf16[768,1152]{1,0:T(8,128)(2,1)}, u32[]{:S(2)}) copy-start(bf16[768,1152]{1,0:T(8,128)(2,1)} %refs_9_.1) | copy-start | bytes 5308420
  1.8 2.5 %copy-start.1 = (bf16[8,32,768]{2,1,0:T(8,128)(2,1)S(1)}, bf16[8,32,768]{2,1,0:T(8,128)(2,1)}, u32[]{:S(2)}) copy-start(bf16[8,32,768]{2,1,0:T(8,128)(2,1)} %param.5) | copy-start | bytes 1179652
  1.8 2.5 %copy-start.2 = (bf16[8,32,384]{2,1,0:T(8,128)(2,1)S(1)}, bf16[8,32,384]{2,1,0:T(8,128)(2,1)}, u32[]{:S(2)}) copy-start(bf16[8,32,384]{2,1,0:T(8,128)(2,1)} %param.7) | copy-start | bytes 589828

commit v4 on v3

--- a/solution.py
+++ b/solution.py
@@ -173,7 +173,7 @@
 
     lax.fori_loop(0, groups, one_group, 0)
     if more is not None:
-        more.forward()
+        more.early()
 
     def collect(grp, carry):
         for i, d in enumerate(DIRS):
@@ -248,7 +248,7 @@
 
 
 def weight_kernel(
-    nn, ne, mid, tok_ref, dq_ref, out_ref, recv, part, slots,
+    nn, ne, base, tok_ref, dq_ref, out_ref, recv, part, slots,
     a_send, a_recv, r_send, r_recv, z_send, z_recv, p_send, p_recv, f_send, f_recv,
 ):
     e, n = lax.axis_index("ew"), lax.axis_index("ns")
@@ -261,7 +261,7 @@
     sibling = n + 1 - 2 * core
 
     def rows_of(d):
-        return pl.ds(pl.multiple_of(d * share, 16), share)
+        return pl.ds(pl.multiple_of(base + d * share, 16), share)
 
     def at(d, m):
         return (d, m)
@@ -285,7 +285,7 @@
     for k in range(1, nn):
         exchange(k).start()
     recv[n] = dq_ref[rows_of(n), :]
-    mid()
+    yield
     for k in range(1, nn):
         arrived(k).wait_recv()
 
@@ -310,6 +310,8 @@
         def _():
             reduce_copy(c, e).start()
 
+    yield
+
     def spot(c, m):
         return out_ref.at[rows_of(m), c * CH : (c + 1) * CH]
 
@@ -349,6 +351,7 @@
                 column_copy(c, k).start()
             spread(c)
 
+    yield
     for c in order:
 
         @pl.when(e != owner[c])
@@ -356,12 +359,14 @@
             column_copy(c, 1).wait_recv()
             spread(c)
 
+    yield
     for c in order:
         for k in range(1, nn // 2):
             m = peers(k)
             plane_copy(c, m, sibling, p_send, 0, p_recv).wait_recv()
             plane_copy(c, m, sibling, f_send, k, f_recv).start()
 
+    yield
     for c in order:
         plane_copy(c, sibling, sibling, p_send, 0, p_recv).wait_recv()
         for k in range(1, nn // 2):
@@ -426,19 +431,41 @@
             self.pass_on(k, self.peer(k), self.t_recv).wait_recv()
             self.pass_on(k, self.peer(k), self.u_recv).start()
 
+    def early(self):
+        half = len(self.rest) // 2
+        width = self.turned.shape[0] // 3
+        make = lambda base, rest: weight_kernel(
+            self.nn, self.ne, base, self.everything, self.turned, self.gw, *rest
+        )
+        self.parts = [make(0, self.rest[:half]), make(width, self.rest[half:])]
+        next(self.parts[0])
+        self.forward()
+
+    def tokens_in(self):
+        self.pass_on(0, self.sibling, self.t_recv).wait_recv()
+        for k in range(1, self.nn // 2):
+            m = lax.rem(self.sibling + 2 * k, self.nn)
+            self.pass_on(k, m, self.u_recv).wait_recv()
+
     def mid(self):
         dq = self.dqkv[...].reshape(self.count, self.dqkv.shape[2])
         for c in range(0, self.w.shape[0], 256):
             self.gt[:, c : c + 256] = lax.dot_general(
                 dq, self.w[c : c + 256, :], (((1,), (1,)), ((), ())), preferred_element_type=jnp.float32
             ).astype(jnp.bfloat16)
-        self.pass_on(0, self.sibling, self.t_recv).wait_recv()
-        for k in range(1, self.nn // 2):
-            m = lax.rem(self.sibling + 2 * k, self.nn)
-            self.pass_on(k, m, self.u_recv).wait_recv()
 
     def finish(self):
-        weight_kernel(self.nn, self.ne, self.mid, self.everything, self.turned, self.gw, *self.rest)
+        first, second = self.parts
+        next(second)
+        self.tokens_in()
+        next(first)
+        self.mid()
+        next(second)
+        for _ in range(3):
+            next(first)
+            next(second)
+        next(first, None)
+        next(second, None)
         for k in range(self.nn // 2):
             self.send(k).wait_send()
         for k in range(1, self.nn // 2):
@@ -458,8 +485,21 @@
     half, width = RADIUS // 2, total // 3
     groups, side = width // 128, (slots - wide) // 2
     tall = pairs + 2 * half
-    share, chunks = total // nn, features // CH
+    chunks = features // CH
     dma = pltpu.SemaphoreType.DMA
+
+    def weight_scratch(share):
+        return [
+            pltpu.VMEM((nn, share, count), jnp.bfloat16),
+            pltpu.VMEM((chunks, share, CH), jnp.float32),
+            pltpu.VMEM((2, ne, share, CH), jnp.float32),
+            dma((nn,)), dma((nn,)),
+            dma((chunks,)), dma((2, ne)),
+            dma((chunks, ne)), dma((chunks,)),
+            dma((chunks, nn // 2)), dma((chunks, nn)),
+            dma((chunks, nn // 2)), dma((chunks, nn)),
+        ]
+
     vm = pl.BlockSpec(memory_space=pltpu.VMEM)
     back = [
         pltpu.VMEM((groups, half if dn else pairs, side if de else wide, 256), jnp.float32)
@@ -484,15 +524,9 @@
         + back
         + [
             dma((8,)), dma((8,)), dma((8, groups)), dma((8, groups)),
-            pltpu.VMEM((nn, share, count), jnp.bfloat16),
-            pltpu.VMEM((chunks, share, CH), jnp.float32),
-            pltpu.VMEM((2, ne, share, CH), jnp.float32),
-            dma((nn,)), dma((nn,)),
-            dma((chunks,)), dma((2, ne)),
-            dma((chunks, ne)), dma((chunks,)),
-            dma((chunks, nn // 2)), dma((chunks, nn)),
-            dma((chunks, nn // 2)), dma((chunks, nn)),
-        ],
+        ]
+        + weight_scratch(width // nn)
+        + weight_scratch(2 * width // nn),
         compiler_params=pltpu.CompilerParams(
             collective_id=1, has_side_effects=True, vmem_limit_bytes=44 << 20
         ),

time: 94.8 us -> 91.1 us (0.961)
  Pallas kernels: 85.6 us -> 82 us
    pallas_call x1, Pallas kernels: 85.6 us -> 82 us  [fused(): pl.pallas_call(functools.partial(fused_kernel, nn, ne), out_shape=[jax.Sh...]
where the time goes in v4:
time: 91.1 us; the launch traced here: 89.3 us
  Pallas kernels  82 us (90%)
  local copies, waits for them, and re-layouts  3.34 us (4%)
  matrix products  2.43 us (3%)
    pallas_call x1, Pallas kernels, fused(): pl.pallas_call(functools.partial(fused_kernel, nn, ne), out_shape=[jax.Sh...  82 us
    unnamed x8, local copies, waits for them, and re-layouts  2.98 us
    dot_general x1, matrix products, local(): jnp.dot(flat_tokens, w_qkv, preferred_element_type=jnp.float32)  2.43 us

profile of v4, /device:TPU:0, one launch (start us, length us, event | category | flops | bytes accessed | tf_op | source)
XLA Modules:
  0.0 89.3 jit_solution(11416509413276797637)
XLA Ops:
  0.6 0.7 broadcast_add_fusion
  1.4 0.1 stack_reshape.14
  1.4 0.1 stack_reshape.15
  1.5 0.1 stack_reshape.13
  1.6 0.1 stack_reshape.12
  1.7 0.0 copy-start
  1.8 0.0 copy-start.1
  1.8 0.0 copy-start.2
  1.8 2.4 %convolution_convert_fusion = bf16[256,1152]{1,0:T(8,128)(2,1)S(1)} fusion(bf16[256,768]{1,0:T(8,128)(2,1)} %bitcast.15, bf16[768,1152]{1,0:T(8,128)(2,1)} %refs_9_.1), kind=kOutput, calls=%fused_computation | convolution fusion | flops 453279744 | bytes 2752512 | tf_op jit(solution)/shard_map/dot_general | solution.py:548
  4.3 0.0 copy-done
  4.3 0.0 copy-done.1
  4.3 0.0 copy-done.2
  4.3 82.0 %shard_map.68 = (bf16[256,768]{1,0:T(8,128)(2,1)S(1)}, bf16[1152,768]{1,0:T(8,128)(2,1)S(1)}) custom-call(s32[256,1]{1,0:T(8,128)S(1)} %get-tuple-element.18.refs_0_, s32[256,1]{1,0:T(8,128)S(1)} %get-tuple-element.19.refs_1_, s32[2,1,768]{2,1,0:T(1,128)S(1)} %pad_add_fusion.refs_2_, s32[2,1,768]{2,1,0:T(1,128)S(1)} %pad_add_fusion.1.refs_3_, ...), custom_call_target="tpu_custom_call" | custom-call | flops 2227175424 | bytes 8388608 | tf_op jit(solution)/shard_map/pallas_call | solution.py:508
  86.3 2.2 %copy.7 = bf16[768,1152]{1,0:T(8,128)(2,1)} copy(bf16[768,1152]{0,1:T(8,128)(2,1)S(1)} %bitcast.10) | data formatting | bytes 3538944
  88.5 0.7 copy.9
  (6 shorter events, 0.1 us)
Async XLA Ops:
  1.7 2.5 %copy-start = (bf16[768,1152]{1,0:T(8,128)(2,1)S(1)}, bf16[768,1152]{1,0:T(8,128)(2,1)}, u32[]{:S(2)}) copy-start(bf16[768,1152]{1,0:T(8,128)(2,1)} %refs_9_.1) | copy-start | bytes 5308420
  1.8 2.5 %copy-start.1 = (bf16[8,32,768]{2,1,0:T(8,128)(2,1)S(1)}, bf16[8,32,768]{2,1,0:T(8,128)(2,1)}, u32[]{:S(2)}) copy-start(bf16[8,32,768]{2,1,0:T(8,128)(2,1)} %param.5) | copy-start | bytes 1179652
  1.8 2.5 %copy-start.2 = (bf16[8,32,384]{2,1,0:T(8,128)(2,1)S(1)}, bf16[8,32,384]{2,1,0:T(8,128)(2,1)}, u32[]{:S(2)}) copy-start(bf16[8,32,384]{2,1,0:T(8,128)(2,1)} %param.7) | copy-start | bytes 589828

commit v5 on v4

--- a/solution.py
+++ b/solution.py
@@ -49,26 +49,39 @@
     def opposite(i):
         return DIRS.index((-DIRS[i][0], -DIRS[i][1]))
 
-    def forward(i):
+    def lane(grp, j, start=0):
+        return pl.ds(pl.multiple_of(start + j * width + grp * lanes, lanes), lanes)
+
+    def forward(i, grp, j):
         dn, de = DIRS[i]
         rows = own_pairs(dn)
         if de == 0:
-            src = qkv_ref.at[rows, :, pl.ds(width, 2 * width)]
+            src = qkv_ref.at[rows, :, lane(grp, j, width)]
         else:
-            src = (first_ref if de < 0 else last_ref).at[rows]
+            src = (first_ref if de < 0 else last_ref).at[rows, :, lane(grp, j)]
         there = opposite(i)
         a, b = region(DIRS[there])
         return pltpu.make_async_remote_copy(
-            src_ref=src, dst_ref=ext.at[a, b], send_sem=f_send.at[i], recv_sem=f_recv.at[there],
+            src_ref=src, dst_ref=ext.at[a, b, lane(grp, j)],
+            send_sem=f_send.at[i, grp, j], recv_sem=f_recv.at[there, grp, j],
             device_id=(e + de, n + dn), device_id_type=MESH,
         )
 
-    def forward_in(i):
+    def forward_in(i, grp, j):
         a, b = region(DIRS[i])
-        return pltpu.make_async_remote_copy(
-            src_ref=ext.at[a, b], dst_ref=ext.at[a, b], send_sem=f_send.at[i], recv_sem=f_recv.at[i],
+        here = ext.at[a, b, lane(grp, j)]
+        return pltpu.make_async_remote_copy(
+            src_ref=here, dst_ref=here, send_sem=f_send.at[i, grp, j], recv_sem=f_recv.at[i, grp, j],
             device_id=(e + DIRS[i][1], n + DIRS[i][0]), device_id_type=MESH,
         )
+
+    def strips_in(grp):
+        for i, d in enumerate(DIRS):
+
+            @pl.when(exists(d))
+            def _():
+                for j in range(2):
+                    forward_in(i, grp, j).wait_recv()
 
     def backward(i, grp):
         a, b = region(DIRS[i])
@@ -103,11 +116,13 @@
     others = nn - 1 + ne - 1 if more is not None else 0
     pl.semaphore_wait(barrier, others + sum(exists(d).astype(jnp.int32) for d in near))
 
-    for i, d in enumerate(DIRS):
-
-        @pl.when(exists(d))
-        def _():
-            forward(i).start()
+    for grp in range(groups):
+        for i, d in enumerate(DIRS):
+
+            @pl.when(exists(d))
+            def _():
+                for j in range(2):
+                    forward(i, grp, j).start()
 
     ext[pl.ds(half, pairs), pl.ds(0, wide), :] = qkv_ref[:, :, pl.ds(width, 2 * width)]
     acc[...] = jnp.zeros_like(acc)
@@ -118,10 +133,7 @@
         def _():
             ext[a, b, :] = jnp.zeros((a.size, b.size, 2 * width), ext.dtype)
 
-        @pl.when(exists(d))
-        def _():
-            forward_in(i).wait_recv()
-
+    strips_in(0)
     if more is not None:
         more.start()
     nt = (((1,), (1,)), ((), ()))
@@ -130,6 +142,10 @@
     count = step * wide
 
     def one_group(grp, carry):
+        @pl.when(grp > 0)
+        def _():
+            strips_in(grp)
+
         at = pl.multiple_of(grp * lanes, lanes)
         at_v = pl.multiple_of(grp * lanes + width, lanes)
         for b in range(nb):
@@ -206,8 +222,9 @@
 
         @pl.when(exists(d))
         def _():
-            forward(i).wait_send()
             for grp in range(groups):
+                for j in range(2):
+                    forward(i, grp, j).wait_send()
                 backward(i, grp).wait_send()
 
 
@@ -232,7 +249,7 @@
             pltpu.VMEM((groups, tall, slots, 256), jnp.float32),
         ]
         + back
-        + [dma((8,)), dma((8,)), dma((8, groups)), dma((8, groups))],
+        + [dma((8, groups, 2)), dma((8, groups, 2)), dma((8, groups)), dma((8, groups))],
         compiler_params=pltpu.CompilerParams(
             collective_id=2, has_side_effects=True, vmem_limit_bytes=44 << 20
         ),
@@ -523,7 +540,7 @@
         ]
         + back
         + [
-            dma((8,)), dma((8,)), dma((8, groups)), dma((8, groups)),
+            dma((8, groups, 2)), dma((8, groups, 2)), dma((8, groups)), dma((8, groups)),
         ]
         + weight_scratch(width // nn)
         + weight_scratch(2 * width // nn),

time: 91.1 us -> 89.4 us (0.981); the launches traced: 89.3 us -> 88.6 us
  no operation moved by 1% of the time
where the time goes in v5:
time: 89.4 us; the launch traced here: 88.6 us
  Pallas kernels  81.3 us (91%)
  local copies, waits for them, and re-layouts  3.34 us (4%)
  matrix products  2.43 us (3%)
    pallas_call x1, Pallas kernels, fused(): pl.pallas_call(functools.partial(fused_kernel, nn, ne), out_shape=[jax.Sh...  81.3 us
    unnamed x8, local copies, waits for them, and re-layouts  2.98 us
    dot_general x1, matrix products, local(): jnp.dot(flat_tokens, w_qkv, preferred_element_type=jnp.float32)  2.43 us

profile of v5, /device:TPU:0, one launch (start us, length us, event | category | flops | bytes accessed | tf_op | source)
XLA Modules:
  0.0 88.6 jit_solution(724856448354378859)
XLA Ops:
  0.6 0.7 broadcast_add_fusion
  1.4 0.1 stack_reshape.14
  1.4 0.1 stack_reshape.15
  1.5 0.1 stack_reshape.13
  1.6 0.1 stack_reshape.12
  1.7 0.0 copy-start
  1.8 0.0 copy-start.1
  1.8 0.0 copy-start.2
  1.8 2.4 %convolution_convert_fusion = bf16[256,1152]{1,0:T(8,128)(2,1)S(1)} fusion(bf16[256,768]{1,0:T(8,128)(2,1)} %bitcast.15, bf16[768,1152]{1,0:T(8,128)(2,1)} %refs_9_.1), kind=kOutput, calls=%fused_computation | convolution fusion | flops 453279744 | bytes 2752512 | tf_op jit(solution)/shard_map/dot_general | solution.py:565
  4.3 0.0 copy-done
  4.3 0.0 copy-done.1
  4.3 0.0 copy-done.2
  4.3 81.3 %shard_map.68 = (bf16[256,768]{1,0:T(8,128)(2,1)S(1)}, bf16[1152,768]{1,0:T(8,128)(2,1)S(1)}) custom-call(s32[256,1]{1,0:T(8,128)S(1)} %get-tuple-element.18.refs_0_, s32[256,1]{1,0:T(8,128)S(1)} %get-tuple-element.19.refs_1_, s32[2,1,768]{2,1,0:T(1,128)S(1)} %pad_add_fusion.refs_2_, s32[2,1,768]{2,1,0:T(1,128)S(1)} %pad_add_fusion.1.refs_3_, ...), custom_call_target="tpu_custom_call" | custom-call | flops 2227175424 | bytes 8388608 | tf_op jit(solution)/shard_map/pallas_call | solution.py:525
  85.6 2.2 %copy.7 = bf16[768,1152]{1,0:T(8,128)(2,1)} copy(bf16[768,1152]{0,1:T(8,128)(2,1)S(1)} %bitcast.10) | data formatting | bytes 3538944
  87.8 0.7 copy.9
  (6 shorter events, 0.1 us)
Async XLA Ops:
  1.7 2.5 %copy-start = (bf16[768,1152]{1,0:T(8,128)(2,1)S(1)}, bf16[768,1152]{1,0:T(8,128)(2,1)}, u32[]{:S(2)}) copy-start(bf16[768,1152]{1,0:T(8,128)(2,1)} %refs_9_.1) | copy-start | bytes 5308420
  1.8 2.5 %copy-start.1 = (bf16[8,32,768]{2,1,0:T(8,128)(2,1)S(1)}, bf16[8,32,768]{2,1,0:T(8,128)(2,1)}, u32[]{:S(2)}) copy-start(bf16[8,32,768]{2,1,0:T(8,128)(2,1)} %param.5) | copy-start | bytes 1179652
  1.8 2.5 %copy-start.2 = (bf16[8,32,384]{2,1,0:T(8,128)(2,1)S(1)}, bf16[8,32,384]{2,1,0:T(8,128)(2,1)}, u32[]{:S(2)}) copy-start(bf16[8,32,384]{2,1,0:T(8,128)(2,1)} %param.7) | copy-start | bytes 589828

commit v6 on v5

--- a/solution.py
+++ b/solution.py
@@ -124,6 +124,8 @@
                 for j in range(2):
                     forward(i, grp, j).start()
 
+    if more is not None:
+        more.start()
     ext[pl.ds(half, pairs), pl.ds(0, wide), :] = qkv_ref[:, :, pl.ds(width, 2 * width)]
     acc[...] = jnp.zeros_like(acc)
     for i, d in enumerate(DIRS):
@@ -134,8 +136,6 @@
             ext[a, b, :] = jnp.zeros((a.size, b.size, 2 * width), ext.dtype)
 
     strips_in(0)
-    if more is not None:
-        more.start()
     nt = (((1,), (1,)), ((), ()))
     tn = (((0,), (0,)), ((), ()))
     dot = functools.partial(lax.dot_general, preferred_element_type=jnp.float32)

time: 89.4 us -> 89.4 us (level)
  no operation moved by 1% of the time
where the time goes in v6:
time: 89.4 us; the launch traced here: 88.6 us
  Pallas kernels  81.3 us (91%)
  local copies, waits for them, and re-layouts  3.34 us (4%)
  matrix products  2.43 us (3%)
    pallas_call x1, Pallas kernels, fused(): pl.pallas_call(functools.partial(fused_kernel, nn, ne), out_shape=[jax.Sh...  81.3 us
    unnamed x8, local copies, waits for them, and re-layouts  2.98 us
    dot_general x1, matrix products, local(): jnp.dot(flat_tokens, w_qkv, preferred_element_type=jnp.float32)  2.43 us

profile of v6, /device:TPU:0, one launch (start us, length us, event | category | flops | bytes accessed | tf_op | source)
XLA Modules:
  0.0 88.6 jit_solution(13370463281924677442)
XLA Ops:
  0.6 0.7 broadcast_add_fusion
  1.4 0.1 stack_reshape.14
  1.4 0.1 stack_reshape.15
  1.5 0.1 stack_reshape.13
  1.6 0.1 stack_reshape.12
  1.7 0.0 copy-start
  1.8 0.0 copy-start.1
  1.8 0.0 copy-start.2
  1.8 2.4 %convolution_convert_fusion = bf16[256,1152]{1,0:T(8,128)(2,1)S(1)} fusion(bf16[256,768]{1,0:T(8,128)(2,1)} %bitcast.15, bf16[768,1152]{1,0:T(8,128)(2,1)} %refs_9_.1), kind=kOutput, calls=%fused_computation | convolution fusion | flops 453279744 | bytes 2752512 | tf_op jit(solution)/shard_map/dot_general | solution.py:565
  4.3 0.0 copy-done
  4.3 0.0 copy-done.1
  4.3 0.0 copy-done.2
  4.3 81.3 %shard_map.68 = (bf16[256,768]{1,0:T(8,128)(2,1)S(1)}, bf16[1152,768]{1,0:T(8,128)(2,1)S(1)}) custom-call(s32[256,1]{1,0:T(8,128)S(1)} %get-tuple-element.18.refs_0_, s32[256,1]{1,0:T(8,128)S(1)} %get-tuple-element.19.refs_1_, s32[2,1,768]{2,1,0:T(1,128)S(1)} %pad_add_fusion.refs_2_, s32[2,1,768]{2,1,0:T(1,128)S(1)} %pad_add_fusion.1.refs_3_, ...), custom_call_target="tpu_custom_call" | custom-call | flops 2227175424 | bytes 8388608 | tf_op jit(solution)/shard_map/pallas_call | solution.py:525
  85.6 2.2 %copy.7 = bf16[768,1152]{1,0:T(8,128)(2,1)} copy(bf16[768,1152]{0,1:T(8,128)(2,1)S(1)} %bitcast.10) | data formatting | bytes 3538944
  87.8 0.7 copy.9
  (6 shorter events, 0.1 us)
Async XLA Ops:
  1.7 2.5 %copy-start = (bf16[768,1152]{1,0:T(8,128)(2,1)S(1)}, bf16[768,1152]{1,0:T(8,128)(2,1)}, u32[]{:S(2)}) copy-start(bf16[768,1152]{1,0:T(8,128)(2,1)} %refs_9_.1) | copy-start | bytes 5308420
  1.8 2.5 %copy-start.1 = (bf16[8,32,768]{2,1,0:T(8,128)(2,1)S(1)}, bf16[8,32,768]{2,1,0:T(8,128)(2,1)}, u32[]{:S(2)}) copy-start(bf16[8,32,768]{2,1,0:T(8,128)(2,1)} %param.5) | copy-start | bytes 1179652
  1.8 2.5 %copy-start.2 = (bf16[8,32,384]{2,1,0:T(8,128)(2,1)S(1)}, bf16[8,32,384]{2,1,0:T(8,128)(2,1)}, u32[]{:S(2)}) copy-start(bf16[8,32,384]{2,1,0:T(8,128)(2,1)} %param.7) | copy-start | bytes 589828
